TPU v7x, 32 devices: a whole 2x2x4 slice. The times are simulated.
32 devices in a mesh: dp: 8 (over z, x), head: 4 (over y, core).
Axes of the slice: x: 2, y: 2, z: 4, core: 2. Of those that a mesh axis runs over, the one named last changes fastest.
Arguments:
- latents: bfloat16 [16384, 1280], P(('dp', 'head')), may hold values from -6 to 6
- live_keys: int32 [64], P('dp'), may hold values from 64 to 256, as said below
- cotangent: bfloat16 [16384, 1280], P(('dp', 'head')), may hold values from -6 to 6
- inner_weights: float32 [4, 1280, 1280], P(None, 'dp', 'head'), may hold values from -1 to 1
- outer_weights: float32 [2, 1280, 1280], P(None, 'head', 'dp'), may hold values from -1 to 1
- norm_params: float32 [4, 1280], replicated, may hold values from -1 to 3
- inner_first: float32 [4, 1280, 1280], P(None, 'dp', 'head'), may hold values from -6 to 6
- inner_second: float32 [4, 1280, 1280], P(None, 'dp', 'head'), may hold values from 1.048576 to 4.194304
- inner_average: float32 [4, 1280, 1280], P(None, 'dp', 'head'), may hold values from -0.15625 to 0.15625
- outer_first: float32 [2, 1280, 1280], P(None, 'head', 'dp'), may hold values from -6 to 6
- outer_second: float32 [2, 1280, 1280], P(None, 'head', 'dp'), may hold values from 1.048576 to 4.194304
- outer_average: float32 [2, 1280, 1280], P(None, 'head', 'dp'), may hold values from -0.15625 to 0.15625
- norm_first: float32 [4, 1280], replicated, may hold values from -12 to 12
- norm_second: float32 [4, 1280], replicated, may hold values from 4.194304 to 16.777216
Outputs:
- block_output: bfloat16 [16384, 1280], P(('dp', 'head'))
- latent_grad: bfloat16 [16384, 1280], P(('dp', 'head'))
- grad_norm: float32 [], replicated
- inner_moment: float32 [4, 1280, 1280], P(None, 'dp', 'head')
- inner_square: float32 [4, 1280, 1280], P(None, 'dp', 'head')
- inner_update: float32 [4, 1280, 1280], P(None, 'dp', 'head')
- inner_smooth: float32 [4, 1280, 1280], P(None, 'dp', 'head')
- inner_copy: bfloat16 [4, 1280, 1280], P(None, 'dp', 'head')
- outer_moment: float32 [2, 1280, 1280], P(None, 'head', 'dp')
- outer_square: float32 [2, 1280, 1280], P(None, 'head', 'dp')
- outer_update: float32 [2, 1280, 1280], P(None, 'head', 'dp')
- outer_smooth: float32 [2, 1280, 1280], P(None, 'head', 'dp')
- outer_copy: bfloat16 [2, 1280, 1280], P(None, 'head', 'dp')
- norm_moment: float32 [4, 1280], replicated
- norm_square: float32 [4, 1280], replicated
- norm_update: float32 [4, 1280], replicated
- norm_two_grad: float32 [2, 1280], replicated
Inputs may be any that keep to these rules, and one draw needn't show every extreme that they name: Keys of item i at positions below live_keys[i] take part; in every draw some item has all 256.
All inputs are finite; a program needn't handle non-finite values.
Results may differ from a plain program's by a relative error of at most 0.018.
Values may be sent and summed in bfloat16 or wider, within the bound.
A program may use at most 192 MiB of HBM per device.

v0:
```python
import jax
import jax.numpy as jnp
from jax import lax
from jax.sharding import PartitionSpec as P

HEADS = 8
HS = 160
D = 1280
LAT = 256
STEP = 5


NORM_EPS = 1e-05
MASKED = -1e30
CLIP_RATE = 0.02
ADAM_EPS = 1e-08
DECAY_RATE = 0.1
NORM_RATE = 0.3
SMOOTH_RATE = 0.9


def layer_norm(values, gain_row, bias_row):
    centre = values - jnp.mean(values, axis=-1, keepdims=True)
    spread = jnp.mean(centre * centre, axis=-1, keepdims=True)
    return centre * lax.rsqrt(spread + NORM_EPS) * gain_row + bias_row


def gelu_exact(values):
    return jax.nn.gelu(values, approximate=False)


def split_heads(matrix, item_count, head_count):
    return matrix.reshape(
        item_count, matrix.shape[0] // item_count, head_count, matrix.shape[1] // head_count
    )


def masked_scores(query_heads, key_heads, live_rows):
    scores = jnp.einsum(
        "iqhd,ikhd->ihqk", query_heads, key_heads, preferred_element_type=jnp.float32
    ) * HS ** (-0.5)
    length = key_heads.shape[1]
    valid = lax.broadcasted_iota(jnp.int32, (1, 1, 1, length), 3) < live_rows[:, None, None, None]
    return jnp.where(valid, scores, MASKED)


def attend(projected, live_rows, head_count):
    item_count = live_rows.shape[0]
    query_heads = split_heads(projected[0], item_count, head_count)
    key_heads = split_heads(projected[1], item_count, head_count)
    value_heads = split_heads(projected[2], item_count, head_count)
    scores = masked_scores(query_heads, key_heads, live_rows)
    row_peak = jnp.max(scores, axis=-1, keepdims=True)
    log_total = row_peak + jnp.log(jnp.sum(jnp.exp(scores - row_peak), axis=-1, keepdims=True))
    probs_b = jnp.exp(scores - log_total).astype(jnp.bfloat16)
    attended = jnp.einsum(
        "ihqk,ikhd->iqhd", probs_b, value_heads, preferred_element_type=jnp.float32
    )
    return (
        attended.reshape(projected.shape[1], projected.shape[2]).astype(jnp.bfloat16),
        log_total,
    )


def attend_back(projected, d_attended, log_total, live_rows, head_count):
    item_count = live_rows.shape[0]
    query_heads = split_heads(projected[0], item_count, head_count)
    key_heads = split_heads(projected[1], item_count, head_count)
    value_heads = split_heads(projected[2], item_count, head_count)
    back_heads = split_heads(d_attended, item_count, head_count)
    scores = masked_scores(query_heads, key_heads, live_rows)
    attn_probs = jnp.exp(scores - log_total)
    probs_b = attn_probs.astype(jnp.bfloat16)
    d_value = jnp.einsum("ihqk,iqhd->ikhd", probs_b, back_heads, preferred_element_type=jnp.float32)
    d_probs = jnp.einsum(
        "iqhd,ikhd->ihqk", back_heads, value_heads, preferred_element_type=jnp.float32
    )
    d_scores = (
        attn_probs * (d_probs - jnp.sum(attn_probs * d_probs, axis=-1, keepdims=True))
    ).astype(jnp.bfloat16)
    score_scale = HS ** (-0.5)
    d_query = (
        jnp.einsum("ihqk,ikhd->iqhd", d_scores, key_heads, preferred_element_type=jnp.float32)
        * score_scale
    )
    d_key = (
        jnp.einsum("ihqk,iqhd->ikhd", d_scores, query_heads, preferred_element_type=jnp.float32)
        * score_scale
    )
    flat_shape = projected.shape[1:]
    return jnp.stack(
        [d_query.reshape(flat_shape), d_key.reshape(flat_shape), d_value.reshape(flat_shape)]
    ).astype(jnp.bfloat16)


def adam_step(weight, grad, first, second, rate, decay):
    moment = 0.5 * first + 0.5 * grad
    square = 0.5 * second + 0.5 * grad * grad
    fix = 1.0 - 0.5**STEP
    update = weight - rate * (moment / fix / (jnp.sqrt(square / fix) + ADAM_EPS) + decay * weight)
    return (moment, square, update)


def shards(
    latents,
    live_keys,
    cotangent,
    inner_weights,
    outer_weights,
    norm_params,
    inner_first,
    inner_second,
    inner_average,
    outer_first,
    outer_second,
    outer_average,
    norm_first,
    norm_second,
):
    head_devices = lax.axis_size("head")
    data_devices = lax.axis_size("dp")
    row_count = latents.shape[0]
    inner_b, outer_b = (
        lax.all_gather(inner_weights.astype(jnp.bfloat16), "dp", axis=1, tiled=True),
        lax.all_gather(outer_weights.astype(jnp.bfloat16), "dp", axis=2, tiled=True),
    )
    source = latents.astype(jnp.float32)
    normed = layer_norm(source, norm_params[0], norm_params[1]).astype(jnp.bfloat16)
    qkv_b = inner_b[:3]
    proj_b = outer_b[0]
    head_count = HEADS // head_devices
    normed_all = lax.all_gather(normed, "head", axis=0, tiled=True)
    up_b = inner_b[3]
    down_b = outer_b[1]
    projected = jnp.einsum(
        "rd,tdc->trc", normed_all, qkv_b, preferred_element_type=jnp.float32
    ).astype(jnp.bfloat16)
    attended, log_total = attend(projected, live_keys, head_count)
    attn_part = lax.psum_scatter(
        jnp.dot(attended, proj_b, preferred_element_type=jnp.float32),
        "head",
        scatter_dimension=0,
        tiled=True,
    )
    residual = source + attn_part
    normed_two = layer_norm(residual, norm_params[2], norm_params[3]).astype(jnp.bfloat16)
    normed_two_all = lax.all_gather(normed_two, "head", axis=0, tiled=True)
    preact = jnp.dot(normed_two_all, up_b, preferred_element_type=jnp.float32)
    activation = gelu_exact(preact).astype(jnp.bfloat16)
    mlp_part = lax.psum_scatter(
        jnp.dot(activation, down_b, preferred_element_type=jnp.float32).astype(jnp.bfloat16),
        "head",
        scatter_dimension=0,
        tiled=True,
    ).astype(jnp.float32)
    block_output = (residual + mlp_part).astype(jnp.bfloat16)
    back_all = lax.all_gather(cotangent, "head", axis=0, tiled=True)
    grad_down = jnp.einsum("rc,rd->cd", activation, back_all, preferred_element_type=jnp.float32)
    d_activ = jnp.einsum("rd,cd->rc", back_all, down_b, preferred_element_type=jnp.float32)
    gelu_back = jax.vjp(gelu_exact, preact)[1]
    d_pre = gelu_back(d_activ)[0].astype(jnp.bfloat16)
    grad_up = jnp.einsum("rd,rc->dc", normed_two_all, d_pre, preferred_element_type=jnp.float32)
    d_normed_two = lax.psum_scatter(
        jnp.einsum("rc,dc->rd", d_pre, up_b, preferred_element_type=jnp.float32),
        "head",
        scatter_dimension=0,
        tiled=True,
    )
    norm_back_two = jax.vjp(layer_norm, residual, norm_params[2], norm_params[3])[1]
    d_resid_norm, grad_gain_two, grad_bias_two = norm_back_two(d_normed_two)
    d_resid = cotangent.astype(jnp.float32) + d_resid_norm
    d_resid_b = d_resid.astype(jnp.bfloat16)
    d_resid_all = lax.all_gather(d_resid_b, "head", axis=0, tiled=True)
    grad_outproj = jnp.einsum(
        "rc,rd->cd", attended, d_resid_all, preferred_element_type=jnp.float32
    )
    d_attended = jnp.einsum(
        "rd,cd->rc", d_resid_all, proj_b, preferred_element_type=jnp.float32
    ).astype(jnp.bfloat16)
    d_proj = attend_back(projected, d_attended, log_total, live_keys, head_count)
    grad_qkv = jnp.einsum("rd,trc->tdc", normed_all, d_proj, preferred_element_type=jnp.float32)
    d_normed = lax.psum_scatter(
        jnp.einsum("trc,tdc->rd", d_proj, qkv_b, preferred_element_type=jnp.float32).astype(
            jnp.bfloat16
        ),
        "head",
        scatter_dimension=0,
        tiled=True,
    ).astype(jnp.float32)
    norm_back_one = jax.vjp(layer_norm, source, norm_params[0], norm_params[1])[1]
    d_source_norm, grad_gain_one, grad_bias_one = norm_back_one(d_normed)
    latent_grad = (d_resid + d_source_norm).astype(jnp.bfloat16)
    grad_inner = jnp.concatenate([grad_qkv, grad_up[None]], axis=0)
    grad_outer = jnp.stack([grad_outproj, grad_down])
    grad_inner, grad_outer = (
        lax.psum_scatter(
            grad_inner.astype(jnp.bfloat16), "dp", scatter_dimension=1, tiled=True
        ).astype(jnp.float32),
        lax.psum_scatter(
            grad_outer.astype(jnp.bfloat16), "dp", scatter_dimension=2, tiled=True
        ).astype(jnp.float32),
    )
    norm_part = jnp.stack([grad_gain_one, grad_bias_one, grad_gain_two, grad_bias_two])
    local_squares = jnp.sum(grad_inner * grad_inner) + jnp.sum(grad_outer * grad_outer)
    grad_norms, squares_all = lax.psum((norm_part, local_squares), ("dp", "head"))
    grad_norm = jnp.sqrt(squares_all + jnp.sum(grad_norms * grad_norms))
    token_total = row_count * head_devices * data_devices
    clip_limit = CLIP_RATE * D * token_total**0.5
    factor = jnp.minimum(1.0, clip_limit / grad_norm)
    inner_rate = D ** (-0.5)
    outer_rate = jnp.array([(LAT / (3.0 * D)) ** 0.5, D ** (-0.5)], dtype=jnp.float32).reshape(
        2, 1, 1
    )
    clipped_norms = grad_norms * factor
    inner_new = adam_step(
        inner_weights, grad_inner * factor, inner_first, inner_second, inner_rate, DECAY_RATE
    )
    outer_new = adam_step(
        outer_weights, grad_outer * factor, outer_first, outer_second, outer_rate, DECAY_RATE
    )
    norm_new = adam_step(norm_params, clipped_norms, norm_first, norm_second, NORM_RATE, 0.0)
    inner_smooth = SMOOTH_RATE * inner_average + (1.0 - SMOOTH_RATE) * inner_new[2]
    outer_smooth = SMOOTH_RATE * outer_average + (1.0 - SMOOTH_RATE) * outer_new[2]
    return (
        block_output,
        latent_grad,
        grad_norm,
        inner_new[0],
        inner_new[1],
        inner_new[2],
        inner_smooth,
        inner_new[2].astype(jnp.bfloat16),
        outer_new[0],
        outer_new[1],
        outer_new[2],
        outer_smooth,
        outer_new[2].astype(jnp.bfloat16),
        norm_new[0],
        norm_new[1],
        norm_new[2],
        clipped_norms[2:4],
    )


def solution(mesh):
    return jax.shard_map(
        shards,
        mesh=mesh,
        in_specs=(
            P(("dp", "head"), None),
            P("dp"),
            P(("dp", "head"), None),
            P(None, "dp", "head"),
            P(None, "head", "dp"),
            P(),
            P(None, "dp", "head"),
            P(None, "dp", "head"),
            P(None, "dp", "head"),
            P(None, "head", "dp"),
            P(None, "head", "dp"),
            P(None, "head", "dp"),
            P(),
            P(),
        ),
        out_specs=(
            P(("dp", "head"), None),
            P(("dp", "head"), None),
            P(),
            P(None, "dp", "head"),
            P(None, "dp", "head"),
            P(None, "dp", "head"),
            P(None, "dp", "head"),
            P(None, "dp", "head"),
            P(None, "head", "dp"),
            P(None, "head", "dp"),
            P(None, "head", "dp"),
            P(None, "head", "dp"),
            P(None, "head", "dp"),
            P(),
            P(),
            P(),
            P(),
        ),
        check_vma=False,
    )
```

profile of v0, /device:TPU:0, one launch (start us, length us, event | category | flops | bytes accessed | tf_op | source)
XLA Modules:
  0.0 926.1 jit_solution(11313431525313861724)
XLA Ops:
  14.4 69.2 %all-gather.9.cloned.1.call-done = bf16[4,1280,320]{2,0,1:T(4,128)(2,1)} async-done(((bf16[4,160,320]{2,0,1:T(4,128)(2,1)}), bf16[4,1280,320]{2,0,1:T(4,128)(2,1)}) %all-gather.9.cloned.1.call-update) | async-done | bytes 3276816 | tf_op jit(solution)/shard_map/all_gather | solution.py:124
  83.6 7.2 copy.210
  90.9 33.7 %all-gather.7.cloned.1.call-done = bf16[2048,1280]{1,0:T(8,128)(2,1)} async-done(((bf16[512,1280]{1,0:T(8,128)(2,1)}), bf16[2048,1280]{1,0:T(8,128)(2,1)}) %all-gather.7.cloned.1.call-update) | async-done | bytes 5242896 | tf_op jit(solution)/shard_map/all_gather | solution.py:132
  124.6 8.0 convert_bitcast_fusion
  140.4 34.5 %all-gather.11.cloned.1.call-done = bf16[2,320,1280]{1,2,0:T(8,128)(2,1)} async-done(((bf16[2,320,160]{1,2,0:T(8,128)(2,1)}), bf16[2,320,1280]{1,2,0:T(8,128)(2,1)}) %all-gather.11.cloned.1.call-update) | async-done | bytes 1638416 | tf_op jit(solution)/shard_map/all_gather | solution.py:125
  174.9 6.8 fusion.52
  181.8 84.5 %reduce-scatter.5.cloned.1.call-done = f32[512,1280]{1,0:T(8,128)} async-done(((f32[2048,1280]{1,0:T(8,128)}), f32[512,1280]{1,0:T(8,128)}) %reduce-scatter.5.cloned.1.call-update) | async-done | bytes 2621456 | tf_op jit(solution)/shard_map/reduce_scatter | solution.py:139
  281.0 30.3 %all-gather.13.cloned.1.call-done = bf16[2048,1280]{1,0:T(8,128)(2,1)} async-done(((bf16[512,1280]{1,0:T(8,128)(2,1)}), bf16[2048,1280]{1,0:T(8,128)(2,1)}) %all-gather.13.cloned.1.call-update) | async-done | bytes 5242896 | tf_op jit(solution)/shard_map/all_gather | solution.py:147
  311.3 10.6 %multiply_convert_fusion.3 = (bf16[2048,320]{0,1:T(8,128)(2,1)}, f32[2048,320]{0,1:T(8,128)}, f32[2048,320]{0,1:T(8,128)}) fusion(bf16[2048,1280]{1,0:T(8,128)(2,1)} %all-gather.13.cloned.1.call-done, bf16[1,1280,320]{1,2,0:T(8,128)(2,1)S(1)} %copy.211), kind=kOutput, calls=%fused_computation.49 | convolution fusion | flops 1720320000 | bytes 12615680 | tf_op jit(solution)/shard_map/dot_general | solution.py:148
  321.9 31.3 %all-gather.15.cloned.1.call-done = bf16[2048,1280]{1,0:T(8,128)(2,1)} async-done(((bf16[512,1280]{1,0:T(8,128)(2,1)}), bf16[2048,1280]{1,0:T(8,128)(2,1)}) %all-gather.15.cloned.1.call-update) | async-done | bytes 5242896 | tf_op jit(solution)/shard_map/all_gather | solution.py:157
  353.2 7.0 add_convert_fusion.1
  361.3 5.6 fusion.54
  366.9 7.2 convolution_convert_fusion
  374.3 78.1 %reduce-scatter.9.cloned.1.call-done = f32[512,1280]{1,0:T(8,128)} async-done(((f32[2048,1280]{1,0:T(8,128)}), f32[512,1280]{1,0:T(8,128)}) %reduce-scatter.9.cloned.1.call-update) | async-done | bytes 2621456 | tf_op jit(solution)/shard_map/reduce_scatter | solution.py:163
  455.0 51.4 %reduce-scatter.7.cloned.1.call-done = bf16[512,1280]{1,0:T(8,128)(2,1)} async-done(((bf16[2048,1280]{1,0:T(8,128)(2,1)}), bf16[512,1280]{1,0:T(8,128)(2,1)}) %reduce-scatter.7.cloned.1.call-update) | async-done | bytes 1310736 | tf_op jit(solution)/shard_map/reduce_scatter | solution.py:150
  513.6 5.3 fusion.31
  519.0 6.0 fusion.32
  524.9 29.2 %all-gather.17.cloned.1.call-done = bf16[2048,1280]{1,0:T(8,128)(2,1)} async-done(((bf16[512,1280]{1,0:T(8,128)(2,1)}), bf16[2048,1280]{1,0:T(8,128)(2,1)}) %all-gather.17.cloned.1.call-update) | async-done | bytes 5242896 | tf_op jit(solution)/shard_map/all_gather | solution.py:173
  589.9 9.4 %fusion.14 = bf16[3,1280,320]{1,2,0:T(8,128)(2,1)S(1)} fusion(bf16[3,2048,320]{1,2,0:T(8,128)(2,1)S(1)} %constant_dynamic-update-slice_fusion, bf16[2048,1280]{1,0:T(8,128)(2,1)} %all-gather.7.cloned.1.call-done), kind=kOutput, calls=%fused_computation.28 | convolution fusion | flops 5034393600 | bytes 11632640 | tf_op jit(solution)/shard_map/rd,trc->tdc/dot_general | solution.py:181
  599.6 6.5 copy.202
  607.8 10.7 %bitcast_convert_fusion = bf16[2048,1280]{1,0:T(8,128)(2,1)} fusion(bf16[3,2048,320]{1,2,0:T(8,128)(2,1)} %copy-done.34, bf16[3,1280,320]{1,2,0:T(8,128)(2,1)S(1)} %copy-done.20), kind=kOutput, calls=%fused_computation | convolution fusion | flops 5035786240 | bytes 11632640 | tf_op jit(solution)/shard_map/trc,tdc->rd/dot_general | solution.py:183
  620.4 187.7 %all-reduce.6.cloned.1.call-done = (bf16[4,1280,320]{2,0,1:T(4,128)(2,1)}, bf16[2,320,1280]{1,0,2:T(2,128)(2,1)}) async-done(((bf16[4,1280,320]{2,0,1:T(4,128)(2,1)}, bf16[2,320,1280]{1,0,2:T(2,128)(2,1)}), (bf16[4,1280,320]{2,0,1:T(4,128)(2,1)}, bf16[2,320,1280]{1,0,2:T(2,128)(2,1)})) %all-reduce.6.cloned.1.call-update) | async-done | bytes 4915216
  813.3 47.7 %reduce-scatter.11.cloned.1.call-done = bf16[512,1280]{1,0:T(8,128)(2,1)} async-done(((bf16[2048,1280]{1,0:T(8,128)(2,1)}), bf16[512,1280]{1,0:T(8,128)(2,1)}) %reduce-scatter.11.cloned.1.call-update) | async-done | bytes 1310736 | tf_op jit(solution)/shard_map/reduce_scatter | solution.py:182
  864.5 39.8 %all-reduce.2 = (f32[]{:T(128)}, f32[4,1280]{1,0:T(4,128)S(1)}) all-reduce(f32[]{:T(128)S(6)} %add.148, f32[4,1280]{1,0:T(4,128)S(1)} %pad_maximum_fusion.2), channel_id=1, replica_groups=mesh['dp'=8,'head'=4] {'dp','head'}, use_global_device_ids=true, to_apply=%region_19.20 | all-reduce | flops 5121 | bytes 40968 | tf_op jit(solution)/shard_map/psum | solution.py:205
  (200 shorter events, 98.8 us)
Async XLA Ops:
  7.2 76.4 %all-gather.9.cloned.1.call-start = ((), (), s32[]{:S(2)}) async-start(), calls=%async_computation.5 | async-start | bytes 4423680 | tf_op jit(solution)/shard_map/all_gather | solution.py:124
  10.0 114.6 %all-gather.7.cloned.1.call-start = ((), (), s32[]{:S(2)}) async-start(), calls=%async_computation.4 | async-start | bytes 6553600 | tf_op jit(solution)/shard_map/all_gather | solution.py:132
  11.8 79.1 %copy-start.44 = (f32[512]{0:T(512)}, f32[512]{0:T(512)S(1)}, u32[]{:S(2)}) copy-start(f32[512]{0:T(512)S(1)} %fusion.21) | copy-start | bytes 6148
  11.8 79.1 %copy-start.40 = (f32[512]{0:T(512)}, f32[512]{0:T(512)S(1)}, u32[]{:S(2)}) copy-start(f32[512]{0:T(512)S(1)} %fusion.63) | copy-start | bytes 6148
  13.4 161.5 %all-gather.11.cloned.1.call-start = ((), (), s32[]{:S(2)}) async-start(), calls=%async_computation.6 | async-start | bytes 2211840 | tf_op jit(solution)/shard_map/all_gather | solution.py:125
  14.3 252.0 %reduce-scatter.5.cloned.1.call-start = ((), (), s32[]{:S(2)}) async-start(), calls=%async_computation.7 | async-start | bytes 13107200 | tf_op jit(solution)/shard_map/reduce_scatter | solution.py:139
  90.9 41.7 %copy-start.19 = (bf16[3,1280,320]{1,2,0:T(8,128)(2,1)}, bf16[3,1280,320]{1,2,0:T(8,128)(2,1)S(1)}, u32[]{:S(2)}) copy-start(bf16[3,1280,320]{1,2,0:T(8,128)(2,1)S(1)} %copy.210) | copy-start | bytes 7372804
  140.4 41.3 %copy-start.11 = (bf16[40,8,8,256]{3,1,2,0:T(8,128)(2,1)}, bf16[40,8,8,256]{3,1,2,0:T(8,128)(2,1)S(1)}, u32[]{:S(2)}) copy-start(bf16[40,8,8,256]{3,1,2,0:T(8,128)(2,1)S(1)} %copy.215) | copy-start | bytes 3932164
  181.7 129.6 %all-gather.13.cloned.1.call-start = ((), (), s32[]{:S(2)}) async-start(), calls=%async_computation.8 | async-start | bytes 6553600 | tf_op jit(solution)/shard_map/all_gather | solution.py:147
  270.7 82.5 %all-gather.15.cloned.1.call-start = ((), (), s32[]{:S(2)}) async-start(), calls=%async_computation.10 | async-start | bytes 6553600 | tf_op jit(solution)/shard_map/all_gather | solution.py:157
  271.3 181.2 %reduce-scatter.9.cloned.1.call-start = ((), (), s32[]{:S(2)}) async-start(), calls=%async_computation.11 | async-start | bytes 13107200 | tf_op jit(solution)/shard_map/reduce_scatter | solution.py:163
  366.9 139.5 %reduce-scatter.7.cloned.1.call-start = ((), (), s32[]{:S(2)}) async-start(), calls=%async_computation.9 | async-start | bytes 6553600 | tf_op jit(solution)/shard_map/reduce_scatter | solution.py:150
  374.1 180.0 %all-gather.17.cloned.1.call-start = ((), (), s32[]{:S(2)}) async-start(), calls=%async_computation.12 | async-start | bytes 6553600 | tf_op jit(solution)/shard_map/all_gather | solution.py:173
  513.6 294.5 %all-reduce.6.cloned.1.call-start = ((), (), s32[]{:S(2)}) async-start(), calls=%async_computation.14 | async-start | bytes 11796480
  606.1 254.9 %reduce-scatter.11.cloned.1.call-start = ((), (), s32[]{:S(2)}) async-start(), calls=%async_computation.13 | async-start | bytes 6553600 | tf_op jit(solution)/shard_map/reduce_scatter | solution.py:182
  618.5 242.6 %copy-start.1 = (bf16[512,1280]{1,0:T(8,128)(2,1)S(1)}, bf16[512,1280]{1,0:T(8,128)(2,1)}, u32[]{:S(2)}) copy-start(bf16[512,1280]{1,0:T(8,128)(2,1)} %param.15) | copy-start | bytes 3932164
  618.5 242.6 %copy-start.36 = (f32[1280]{0:T(1024)S(1)}, f32[1280]{0:T(1024)}, u32[]{:S(2)}) copy-start(f32[1280]{0:T(1024)} %copy-done.35) | copy-start | bytes 15364
  618.5 242.6 %copy-start.39 = (f32[512]{0:T(512)S(1)}, f32[512]{0:T(512)}, u32[]{:S(2)}) copy-start(f32[512]{0:T(512)} %copy-done.38) | copy-start | bytes 6148
  618.5 244.6 %copy-start.45 = (f32[512]{0:T(512)S(1)}, f32[512]{0:T(512)}, u32[]{:S(2)}) copy-start(f32[512]{0:T(512)} %copy-done.44) | copy-start | bytes 6148
  618.5 244.6 %copy-start.41 = (f32[512]{0:T(512)S(1)}, f32[512]{0:T(512)}, u32[]{:S(2)}) copy-start(f32[512]{0:T(512)} %copy-done.40) | copy-start | bytes 6148
  813.3 93.0 %copy-start.37 = (f32[4,1280]{1,0:T(4,128)S(1)}, f32[4,1280]{1,0:T(4,128)}, u32[]{:S(2)}) copy-start(f32[4,1280]{1,0:T(4,128)} %param.20) | copy-start | bytes 61444
  813.3 93.0 %copy-start.42 = (f32[4,1280]{1,0:T(4,128)S(1)}, f32[4,1280]{1,0:T(4,128)}, u32[]{:S(2)}) copy-start(f32[4,1280]{1,0:T(4,128)} %param.28) | copy-start | bytes 61444
  813.3 93.0 %copy-start.43 = (f32[4,1280]{1,0:T(4,128)S(1)}, f32[4,1280]{1,0:T(4,128)}, u32[]{:S(2)}) copy-start(f32[4,1280]{1,0:T(4,128)} %param.27) | copy-start | bytes 61444
  813.3 94.3 %copy-start.46 = (f32[2]{0:T(128)S(1)}, f32[2]{0:T(128)}, u32[]{:S(2)}) copy-start(f32[2]{0:T(128)} %constant.117.clone) | copy-start | bytes 28
  (39 other events, 156.2 us)
Sparse Core Ops, SparseCore 0:
  10.8 72.7 all-gather.8
  85.8 38.7 all-gather.6
  127.4 47.5 all-gather.10
  181.8 84.3 reduce-scatter.4
  270.8 40.4 all-gather.12
  312.7 40.4 all-gather.14
  367.0 85.3 reduce-scatter.8
  455.0 51.3 reduce-scatter.6
  513.7 40.4 all-gather.16
  606.3 201.7 all-reduce.5
  810.6 50.3 reduce-scatter.10
where the time goes:
time: 936 us; the launch traced here: 926 us
  waiting for transfers between devices  678 us (72%)
  matrix products  94.1 us (10%)
  local copies, waits for them, and re-layouts  59.3 us (6%)
  blocking collectives  39.8 us (4%)
  other arithmetic  33.9 us (4%)
  between operations  19.6 us (2%)
    unnamed x12, waiting for transfers between devices  188 us
    reduce_scatter x1, waiting for transfers between devices, shards(): lax.psum_scatter(jnp.dot(attended, proj_b, preferred_element_type=jnp.flo...  84.5 us
    reduce_scatter x1, waiting for transfers between devices, shards(): lax.psum_scatter(jnp.einsum('rc,dc->rd', d_pre, up_b, preferred_element_t...  78.1 us
    all_gather x1, waiting for transfers between devices, shards(): lax.all_gather(inner_weights.astype(jnp.bfloat16), 'dp', axis=1, tiled=True)  69.2 us
    reduce_scatter x1, waiting for transfers between devices, shards(): lax.psum_scatter(jnp.dot(activation, down_b, preferred_element_type=jnp.f...  51.4 us
    reduce_scatter x1, waiting for transfers between devices, shards(): lax.psum_scatter(jnp.einsum('trc,tdc->rd', d_proj, qkv_b, preferred_eleme...  47.7 us
    psum x1, blocking collectives, shards(): lax.psum((norm_part, local_squares), ('dp', 'head'))  39.8 us
    all_gather x1, waiting for transfers between devices, shards(): lax.all_gather(outer_weights.astype(jnp.bfloat16), 'dp', axis=2, tiled=True)  34.5 us
  transfers between devices with their start and end apart: 11, of which 11 were waited for; matrix products, arithmetic and copies ran while one was open for 9% of the time, Pallas kernels for 0%

commit v1 on v0

--- a/solution.py
+++ b/solution.py
@@ -120,73 +120,52 @@
     head_devices = lax.axis_size("head")
     data_devices = lax.axis_size("dp")
     row_count = latents.shape[0]
+    item_count = row_count // LAT
     inner_b, outer_b = (
-        lax.all_gather(inner_weights.astype(jnp.bfloat16), "dp", axis=1, tiled=True),
-        lax.all_gather(outer_weights.astype(jnp.bfloat16), "dp", axis=2, tiled=True),
-    )
+        lax.all_gather(
+            lax.all_gather(inner_weights.astype(jnp.bfloat16), "dp", axis=1, tiled=True),
+            "head", axis=2, tiled=True),
+        lax.all_gather(
+            lax.all_gather(outer_weights.astype(jnp.bfloat16), "dp", axis=2, tiled=True),
+            "head", axis=1, tiled=True),
+    )
+    live_own = lax.dynamic_slice(
+        live_keys, (lax.axis_index("head") * item_count,), (item_count,))
     source = latents.astype(jnp.float32)
     normed = layer_norm(source, norm_params[0], norm_params[1]).astype(jnp.bfloat16)
     qkv_b = inner_b[:3]
     proj_b = outer_b[0]
-    head_count = HEADS // head_devices
-    normed_all = lax.all_gather(normed, "head", axis=0, tiled=True)
     up_b = inner_b[3]
     down_b = outer_b[1]
     projected = jnp.einsum(
-        "rd,tdc->trc", normed_all, qkv_b, preferred_element_type=jnp.float32
-    ).astype(jnp.bfloat16)
-    attended, log_total = attend(projected, live_keys, head_count)
-    attn_part = lax.psum_scatter(
-        jnp.dot(attended, proj_b, preferred_element_type=jnp.float32),
-        "head",
-        scatter_dimension=0,
-        tiled=True,
-    )
-    residual = source + attn_part
+        "rd,tdc->trc", normed, qkv_b, preferred_element_type=jnp.float32
+    ).astype(jnp.bfloat16)
+    attended, log_total = attend(projected, live_own, HEADS)
+    residual = source + jnp.dot(attended, proj_b, preferred_element_type=jnp.float32)
     normed_two = layer_norm(residual, norm_params[2], norm_params[3]).astype(jnp.bfloat16)
-    normed_two_all = lax.all_gather(normed_two, "head", axis=0, tiled=True)
-    preact = jnp.dot(normed_two_all, up_b, preferred_element_type=jnp.float32)
+    preact = jnp.dot(normed_two, up_b, preferred_element_type=jnp.float32)
     activation = gelu_exact(preact).astype(jnp.bfloat16)
-    mlp_part = lax.psum_scatter(
-        jnp.dot(activation, down_b, preferred_element_type=jnp.float32).astype(jnp.bfloat16),
-        "head",
-        scatter_dimension=0,
-        tiled=True,
-    ).astype(jnp.float32)
+    mlp_part = jnp.dot(activation, down_b, preferred_element_type=jnp.float32)
     block_output = (residual + mlp_part).astype(jnp.bfloat16)
-    back_all = lax.all_gather(cotangent, "head", axis=0, tiled=True)
-    grad_down = jnp.einsum("rc,rd->cd", activation, back_all, preferred_element_type=jnp.float32)
-    d_activ = jnp.einsum("rd,cd->rc", back_all, down_b, preferred_element_type=jnp.float32)
+    grad_down = jnp.einsum("rc,rd->cd", activation, cotangent, preferred_element_type=jnp.float32)
+    d_activ = jnp.einsum("rd,cd->rc", cotangent, down_b, preferred_element_type=jnp.float32)
     gelu_back = jax.vjp(gelu_exact, preact)[1]
     d_pre = gelu_back(d_activ)[0].astype(jnp.bfloat16)
-    grad_up = jnp.einsum("rd,rc->dc", normed_two_all, d_pre, preferred_element_type=jnp.float32)
-    d_normed_two = lax.psum_scatter(
-        jnp.einsum("rc,dc->rd", d_pre, up_b, preferred_element_type=jnp.float32),
-        "head",
-        scatter_dimension=0,
-        tiled=True,
-    )
+    grad_up = jnp.einsum("rd,rc->dc", normed_two, d_pre, preferred_element_type=jnp.float32)
+    d_normed_two = jnp.einsum("rc,dc->rd", d_pre, up_b, preferred_element_type=jnp.float32)
     norm_back_two = jax.vjp(layer_norm, residual, norm_params[2], norm_params[3])[1]
     d_resid_norm, grad_gain_two, grad_bias_two = norm_back_two(d_normed_two)
     d_resid = cotangent.astype(jnp.float32) + d_resid_norm
     d_resid_b = d_resid.astype(jnp.bfloat16)
-    d_resid_all = lax.all_gather(d_resid_b, "head", axis=0, tiled=True)
     grad_outproj = jnp.einsum(
-        "rc,rd->cd", attended, d_resid_all, preferred_element_type=jnp.float32
+        "rc,rd->cd", attended, d_resid_b, preferred_element_type=jnp.float32
     )
     d_attended = jnp.einsum(
-        "rd,cd->rc", d_resid_all, proj_b, preferred_element_type=jnp.float32
-    ).astype(jnp.bfloat16)
-    d_proj = attend_back(projected, d_attended, log_total, live_keys, head_count)
-    grad_qkv = jnp.einsum("rd,trc->tdc", normed_all, d_proj, preferred_element_type=jnp.float32)
-    d_normed = lax.psum_scatter(
-        jnp.einsum("trc,tdc->rd", d_proj, qkv_b, preferred_element_type=jnp.float32).astype(
-            jnp.bfloat16
-        ),
-        "head",
-        scatter_dimension=0,
-        tiled=True,
-    ).astype(jnp.float32)
+        "rd,cd->rc", d_resid_b, proj_b, preferred_element_type=jnp.float32
+    ).astype(jnp.bfloat16)
+    d_proj = attend_back(projected, d_attended, log_total, live_own, HEADS)
+    grad_qkv = jnp.einsum("rd,trc->tdc", normed, d_proj, preferred_element_type=jnp.float32)
+    d_normed = jnp.einsum("trc,tdc->rd", d_proj, qkv_b, preferred_element_type=jnp.float32)
     norm_back_one = jax.vjp(layer_norm, source, norm_params[0], norm_params[1])[1]
     d_source_norm, grad_gain_one, grad_bias_one = norm_back_one(d_normed)
     latent_grad = (d_resid + d_source_norm).astype(jnp.bfloat16)
@@ -194,11 +173,13 @@
     grad_outer = jnp.stack([grad_outproj, grad_down])
     grad_inner, grad_outer = (
         lax.psum_scatter(
-            grad_inner.astype(jnp.bfloat16), "dp", scatter_dimension=1, tiled=True
-        ).astype(jnp.float32),
+            lax.psum_scatter(
+                grad_inner.astype(jnp.bfloat16), "head", scatter_dimension=2, tiled=True
+            ), "dp", scatter_dimension=1, tiled=True).astype(jnp.float32),
         lax.psum_scatter(
-            grad_outer.astype(jnp.bfloat16), "dp", scatter_dimension=2, tiled=True
-        ).astype(jnp.float32),
+            lax.psum_scatter(
+                grad_outer.astype(jnp.bfloat16), "head", scatter_dimension=1, tiled=True
+            ), "dp", scatter_dimension=2, tiled=True).astype(jnp.float32),
     )
     norm_part = jnp.stack([grad_gain_one, grad_bias_one, grad_gain_two, grad_bias_two])
     local_squares = jnp.sum(grad_inner * grad_inner) + jnp.sum(grad_outer * grad_outer)

time: 936 us -> 838 us (0.90)
  waiting for transfers between devices: 678 us -> 503 us
  local copies, waits for them, and re-layouts: 59.3 us -> 158 us
  matrix products: 94.1 us -> 79.2 us
    reduce_scatter x4 -> x2, waiting for transfers between devices: 262 us -> 96.1 us  [the longest x1 96 us: shards(): lax.psum_scatter(grad_inner.astype(jnp.bfloat16), 'head', scatter_dimensi...]
    unnamed x117 -> x88, local copies, waits for them, and re-layouts: 27.6 us -> 50.4 us
    all_gather x0 -> x2, local copies, waits for them, and re-layouts: none -> 16.3 us  [the longest x1 8.87 us: shards(): lax.all_gather(inner_weights.astype(jnp.bfloat16), 'dp', axis=1, tiled=True)]
    slice x1 -> x2, local copies, waits for them, and re-layouts: 0.5 us -> 16.3 us  [the longest x1 14.2 us: shards(): down_b = outer_b[1]]
    another operation x4 -> x7, local copies, waits for them, and re-layouts: 6.37 us -> 22 us  [attend_back(): jnp.stack([d_query.reshape(flat_shape), d_key.reshape(flat_shape), d_valu...]
    all_gather x4 -> x2, waiting for transfers between devices: 124 us -> 109 us  [the longest x1 72.3 us: shards(): lax.all_gather(lax.all_gather(inner_weights.astype(jnp.bfloat16), 'dp', a...]
    dot_general x9, matrix products: 59.9 us -> 44.4 us  [the longest x1 9.62 us: shards(): jnp.einsum('rd,tdc->trc', normed, qkv_b, preferred_element_type=jnp.float32)]
    another operation x1 -> x6, local copies, waits for them, and re-layouts: 5.24 us -> 20.3 us  [split_heads(): matrix.reshape(item_count, matrix.shape[0] // item_count, head_count, mat...]
  transfers between devices with their start and end apart: 11 -> 7, of which waited for: 11 -> 6; matrix products, arithmetic and copies ran while one was open for 9% -> 15% of each run, Pallas kernels for 0% -> 0%
where the time goes in v1:
time: 838 us; the launch traced here: 827 us
  waiting for transfers between devices  503 us (60%)
  local copies, waits for them, and re-layouts  158 us (19%)
  matrix products  79.2 us (9%)
  blocking collectives  39.6 us (5%)
  other arithmetic  26.8 us (3%)
  between operations  19.6 us (2%)
    unnamed x8, waiting for transfers between devices  184 us
    reduce_scatter x1, waiting for transfers between devices, shards(): lax.psum_scatter(grad_inner.astype(jnp.bfloat16), 'head', scatter_dimensi...  96 us
    all_gather x1, waiting for transfers between devices, shards(): lax.all_gather(lax.all_gather(inner_weights.astype(jnp.bfloat16), 'dp', a...  72.3 us
    all_gather x1, waiting for transfers between devices, shards(): lax.all_gather(inner_weights.astype(jnp.bfloat16), 'dp', axis=1, tiled=True)  64.4 us
    unnamed x88, local copies, waits for them, and re-layouts  50.4 us
    all_gather x1, waiting for transfers between devices, shards(): lax.all_gather(outer_weights.astype(jnp.bfloat16), 'dp', axis=2, tiled=True)  48.9 us
    psum x1, blocking collectives, shards(): lax.psum((norm_part, local_squares), ('dp', 'head'))  39.6 us
    all_gather x1, waiting for transfers between devices, shards(): lax.all_gather(lax.all_gather(outer_weights.astype(jnp.bfloat16), 'dp', a...  36.6 us
  transfers between devices with their start and end apart: 7, of which 6 were waited for; matrix products, arithmetic and copies ran while one was open for 15% of the time, Pallas kernels for 0%

profile of v1, /device:TPU:0, one launch (start us, length us, event | category | flops | bytes accessed | tf_op | source)
XLA Modules:
  0.0 826.8 jit_solution(10601472068559200581)
XLA Ops:
  12.1 48.9 %all-gather.9.cloned.1.call-done = bf16[2,320,1280]{1,0,2:T(2,128)(2,1)} async-done(((bf16[2,320,160]{1,0,2:T(2,128)(2,1)}), bf16[2,320,1280]{1,0,2:T(2,128)(2,1)}) %all-gather.9.cloned.1.call-update) | async-done | bytes 1638416 | tf_op jit(solution)/shard_map/all_gather | solution.py:129
  61.0 7.5 copy.281
  68.6 64.4 %all-gather.5.cloned.1.call-done = bf16[4,1280,320]{2,0,1:T(4,128)(2,1)} async-done(((bf16[4,160,320]{2,0,1:T(4,128)(2,1)}), bf16[4,1280,320]{2,0,1:T(4,128)(2,1)}) %all-gather.5.cloned.1.call-update) | async-done | bytes 3276816 | tf_op jit(solution)/shard_map/all_gather | solution.py:126
  133.0 8.9 %copy.270 = bf16[4,1280,320]{1,0,2:T(4,128)(2,1)} copy(bf16[4,1280,320]{2,0,1:T(4,128)(2,1)} %all-gather.5.cloned.1.call-done) | data formatting | bytes 6553600 | tf_op jit(solution)/shard_map/all_gather | solution.py:126
  144.2 36.6 %all-gather.11.cloned.1.call-done = bf16[2,1280,1280]{2,0,1:T(2,128)(2,1)} async-done(((bf16[2,320,1280]{2,0,1:T(2,128)(2,1)}), bf16[2,1280,1280]{2,0,1:T(2,128)(2,1)}) %all-gather.11.cloned.1.call-update) | async-done | bytes 6553616 | tf_op jit(solution)/shard_map/all_gather | solution.py:128
  180.8 14.2 %fusion.59 = (bf16[1,1280,1280]{2,0,1:T(2,128)(2,1)}, bf16[1,1280,1280]{2,0,1:T(2,128)(2,1)}) fusion(bf16[2,1280,1280]{2,0,1:T(2,128)(2,1)} %all-gather.11.cloned.1.call-done), kind=kLoop, calls=%fused_computation.133 | loop fusion | bytes 13107200 | tf_op jit(solution)/shard_map/slice | solution.py:139
  195.1 72.3 %all-gather.7.cloned.1.call-done = bf16[4,1280,1280]{1,0,2:T(4,128)(2,1)} async-done(((bf16[4,1280,320]{1,0,2:T(4,128)(2,1)}), bf16[4,1280,1280]{1,0,2:T(4,128)(2,1)}) %all-gather.7.cloned.1.call-update) | async-done | bytes 13107216 | tf_op jit(solution)/shard_map/all_gather | solution.py:125
  267.4 9.7 %slice.58 = bf16[1,1280,1280]{1,0,2:T(2,128)(2,1)} slice(bf16[4,1280,1280]{1,0,2:T(4,128)(2,1)} %all-gather.7.cloned.1.call-done), slice={[3:4], [0:1280], [0:1280]} | slice | bytes 6553600 | tf_op jit(solution)/shard_map/slice | solution.py:138
  277.1 13.6 %copy.328 = bf16[1,1280,1280]{2,1,0:T(8,128)(2,1)} copy(bf16[1,1280,1280]{1,0,2:T(2,128)(2,1)} %slice.58) | data formatting | bytes 6553600
  290.6 19.8 %copy.326 = bf16[3,1280,1280]{2,1,0:T(8,128)(2,1)} copy(bf16[3,1280,1280]{1,0,2:T(4,128)(2,1)} %bitcast.82) | data formatting | bytes 19660800
  310.5 9.6 %fusion.8 = bf16[3,512,1280]{2,1,0:T(8,128)(2,1)S(1)} fusion(bf16[3,1280,1280]{2,1,0:T(8,128)(2,1)} %copy.326, bf16[512,1280]{1,0:T(8,128)(2,1)S(1)} %copy-done.2, f32[1280]{0:T(1024)S(1)} %get-tuple-element.109, f32[1280]{0:T(1024)S(1)} %get-tuple-element.110, f32[512]{0:T(512)S(1)} %fusion.45, f32[512]{0:T(512)S(1)} %broadcast_multiply_fusion.2), kind=kOutput, calls=%fused_computation.26 | convolution fusion | flops 5039063040 | bytes 15087616 | tf_op jit(solution)/shard_map/rd,tdc->trc/dot_general | solution.py:140
  352.9 7.6 multiply_convert_fusion.3
  375.3 5.8 convolution_convert_fusion.5
  388.0 5.1 fusion.31
  399.5 4.7 multiply_reduce_fusion
  432.1 5.9 fusion
  438.0 5.6 pad_maximum_fusion
  443.7 6.7 copy.304
  450.4 96.0 %reduce-scatter.3.cloned.1.call-done = bf16[4,1280,320]{1,2,0:T(8,128)(2,1)} async-done(((bf16[4,1280,1280]{1,2,0:T(8,128)(2,1)}), bf16[4,1280,320]{1,2,0:T(8,128)(2,1)}) %reduce-scatter.3.cloned.1.call-update) | async-done | bytes 3276816 | tf_op jit(solution)/shard_map/reduce_scatter | solution.py:176
  546.5 7.8 copy.302
  556.2 11.7 %fusion.21 = (f32[512]{0:T(512)S(1)}, f32[512,1280]{1,0:T(8,128)S(1)}) fusion(bf16[512,1280]{1,0:T(8,128)(2,1)S(1)} %copy-done.2, f32[1280]{0:T(1024)S(1)} %get-tuple-element.110, f32[512]{0:T(512)S(1)} %broadcast_multiply_fusion.2, bf16[3,512,1280]{2,1,0:T(8,128)(2,1)} %copy-done.22, bf16[3,1280,1280]{2,1,0:T(8,128)(2,1)} %copy.326), kind=kOutput, calls=%fused_computation.44 | convolution fusion | flops 5036441088 | bytes 17703936 | tf_op jit(solution)/shard_map/trc,tdc->rd/dot_general | solution.py:168
  572.2 184.2 %all-reduce.6.cloned.1.call-done = (bf16[4,1280,320]{2,0,1:T(4,128)(2,1)}, bf16[2,320,1280]{1,0,2:T(2,128)(2,1)}) async-done(((bf16[4,1280,320]{2,0,1:T(4,128)(2,1)}, bf16[2,320,1280]{1,0,2:T(2,128)(2,1)}), (bf16[4,1280,320]{2,0,1:T(4,128)(2,1)}, bf16[2,320,1280]{1,0,2:T(2,128)(2,1)})) %all-reduce.6.cloned.1.call-update) | async-done | bytes 4915216
  761.7 7.0 fusion.14
  768.7 39.6 %all-reduce.2 = (f32[]{:T(128)}, f32[4,1280]{1,0:T(4,128)S(1)}) all-reduce(f32[]{:T(128)S(6)} %add.148, f32[4,1280]{1,0:T(4,128)S(1)} %pad_maximum_fusion.2), channel_id=1, replica_groups=mesh['dp'=8,'head'=4] {'dp','head'}, use_global_device_ids=true, to_apply=%region_17.18 | all-reduce | flops 5121 | bytes 40968 | tf_op jit(solution)/shard_map/psum | solution.py:186
  (166 shorter events, 113.7 us)
Async XLA Ops:
  7.2 53.8 %all-gather.9.cloned.1.call-start = ((), (), s32[]{:S(2)}) async-start(), calls=%async_computation.4 | async-start | bytes 2211840 | tf_op jit(solution)/shard_map/all_gather | solution.py:129
  9.4 123.6 %all-gather.5.cloned.1.call-start = ((), (), s32[]{:S(2)}) async-start(), calls=%async_computation.2 | async-start | bytes 4423680 | tf_op jit(solution)/shard_map/all_gather | solution.py:126
  12.1 168.8 %all-gather.11.cloned.1.call-start = ((), (), s32[]{:S(2)}) async-start(), calls=%async_computation.5 | async-start | bytes 8192000 | tf_op jit(solution)/shard_map/all_gather | solution.py:128
  68.5 198.9 %all-gather.7.cloned.1.call-start = ((), (), s32[]{:S(2)}) async-start(), calls=%async_computation.3 | async-start | bytes 16384000 | tf_op jit(solution)/shard_map/all_gather | solution.py:125
  141.9 301.8 %reduce-scatter.5.cloned.1.call-start = ((), (), s32[]{:S(2)}) async-start(), calls=%async_computation.7 | async-start | bytes 8192000 | tf_op jit(solution)/shard_map/reduce_scatter | solution.py:180
  144.2 50.9 %copy-start.27 = (f32[512]{0:T(512)}, f32[512]{0:T(512)S(1)}, u32[]{:S(2)}) copy-start(f32[512]{0:T(512)S(1)} %fusion.20) | copy-start | bytes 6148
  346.4 4.0 slice-start
  352.5 13.2 %copy-start.3 = (f32[512,1280]{1,0:T(8,128)}, f32[512,1280]{1,0:T(8,128)S(1)}, u32[]{:S(2)}) copy-start(f32[512,1280]{1,0:T(8,128)S(1)} %get-tuple-element.140) | copy-start | bytes 7864324
  352.5 8.1 slice-start.2
  352.9 7.7 slice-start.3
  352.9 7.7 copy-start.9
  360.6 9.2 %copy-start.34 = (bf16[512,1280]{1,0:T(8,128)(2,1)}, bf16[512,1280]{1,0:T(8,128)(2,1)S(1)}, u32[]{:S(2)}) copy-start(bf16[512,1280]{1,0:T(8,128)(2,1)S(1)} %get-tuple-element.130) | copy-start | bytes 3932164
  375.1 171.4 %reduce-scatter.3.cloned.1.call-start = ((), (), s32[]{:S(2)}) async-start(), calls=%async_computation.6 | async-start | bytes 16384000 | tf_op jit(solution)/shard_map/reduce_scatter | solution.py:176
  399.5 4.8 copy-start.1
  443.7 312.8 %all-reduce.6.cloned.1.call-start = ((), (), s32[]{:S(2)}) async-start(), calls=%async_computation.8 | async-start | bytes 11796480
  556.2 11.8 %copy-start.28 = (f32[512]{0:T(512)S(1)}, f32[512]{0:T(512)}, u32[]{:S(2)}) copy-start(f32[512]{0:T(512)} %copy-done.27) | copy-start | bytes 6148
  761.6 48.7 %copy-start.24 = (f32[4,1280]{1,0:T(4,128)S(1)}, f32[4,1280]{1,0:T(4,128)}, u32[]{:S(2)}) copy-start(f32[4,1280]{1,0:T(4,128)} %param.20) | copy-start | bytes 61444
  761.7 48.7 %copy-start.25 = (f32[4,1280]{1,0:T(4,128)S(1)}, f32[4,1280]{1,0:T(4,128)}, u32[]{:S(2)}) copy-start(f32[4,1280]{1,0:T(4,128)} %param.28) | copy-start | bytes 61444
  761.7 48.7 %copy-start.26 = (f32[4,1280]{1,0:T(4,128)S(1)}, f32[4,1280]{1,0:T(4,128)}, u32[]{:S(2)}) copy-start(f32[4,1280]{1,0:T(4,128)} %param.27) | copy-start | bytes 61444
  761.7 49.9 %copy-start.16 = (f32[2,320,160]{1,2,0:T(8,128)S(1)}, f32[2,320,160]{1,2,0:T(8,128)}, u32[]{:S(2)}) copy-start(f32[2,320,160]{1,2,0:T(8,128)} %param.19) | copy-start | bytes 1228804
  761.7 49.9 %copy-start.29 = (f32[2]{0:T(128)S(1)}, f32[2]{0:T(128)}, u32[]{:S(2)}) copy-start(f32[2]{0:T(128)} %constant.127.clone) | copy-start | bytes 28
  768.7 46.4 %copy-start.13 = (f32[4,160,320]{2,1,0:T(8,128)S(1)}, f32[4,160,320]{2,1,0:T(8,128)}, u32[]{:S(2)}) copy-start(f32[4,160,320]{2,1,0:T(8,128)} %param.18) | copy-start | bytes 2457604
  768.7 46.4 %copy-start.18 = (f32[4,160,320]{2,1,0:T(8,128)S(1)}, f32[4,160,320]{2,1,0:T(8,128)}, u32[]{:S(2)}) copy-start(f32[4,160,320]{2,1,0:T(8,128)} %param.22) | copy-start | bytes 2457604
  810.3 4.7 copy-start.19
  (22 other events, 42.8 us)
Sparse Core Ops, SparseCore 0:
  10.8 50.1 all-gather.8
  63.8 69.1 all-gather.4
  134.6 46.2 all-gather.10
  182.2 85.0 all-gather.6
  375.2 60.1 reduce-scatter.4
  443.8 102.6 reduce-scatter.2
  554.4 201.9 all-reduce.5

commit v2 on v1

--- a/solution.py
+++ b/solution.py
@@ -1,6 +1,8 @@
 import jax
 import jax.numpy as jnp
 from jax import lax
+from jax.experimental import pallas as pl
+from jax.experimental.pallas import tpu as pltpu
 from jax.sharding import PartitionSpec as P
 
 HEADS = 8
@@ -17,6 +19,169 @@
 DECAY_RATE = 0.1
 NORM_RATE = 0.3
 SMOOTH_RATE = 0.9
+
+
+NM = 6
+MESH = pl.DeviceIdType.MESH
+
+
+def ids():
+    d = lax.axis_index("dp")
+    h = lax.axis_index("head")
+    return d % 2, h // 2, d // 2, h % 2
+
+
+def dev(x, y, z, c):
+    return (z * 2 + x, y * 2 + c)
+
+
+def ag_kernel(sh, w_out, W, sh_in, s0,r0,sz,rz,sa,ra,sb,rb,sd,rd,so):
+    x,y,z,c=ids()
+    sib=dev(x,y,z,1-c); xn=dev(1-x,y,z,c); yn=dev(x,1-y,z,c)
+    zp=[dev(x,y,lax.rem(z+k,4),c) for k in (1,2,3)]
+    bar=pltpu.get_barrier_semaphore()
+    for d in [sib,xn,yn]+zp:
+        pl.semaphore_signal(bar,inc=1,device_id=d,device_id_type=MESH)
+    pl.semaphore_wait(bar,6)
+    yc=pl.ds(pl.multiple_of(y*640,128),640)
+    def rc(src,dst,s,r,d): return pltpu.make_async_remote_copy(src,dst,s,r,device_id=d,device_id_type=MESH)
+    def c0(m): return rc(sh.at[m,1-c], sh_in.at[m], s0.at[m], r0.at[m], sib)
+    unit=lambda m: W.at[m,z,x,c,:,yc]
+    def cz(m,k): return rc(unit(m),unit(m),sz.at[m,k],rz.at[m,k],zp[k])
+    line=lambda m: W.at[m,:,x,c,:,yc]
+    def ca(m,d): return rc(line(m),line(m),sa.at[m],ra.at[m],d)
+    pb0=lambda m: W.at[m,:,:,0,:,yc]
+    pb1=lambda m: W.at[m,:,x,1,:,:]
+    def cb0(m): return rc(pb0(m),pb0(m),sb.at[m],rb.at[m],yn)
+    def cb1(m): return rc(pb1(m),pb1(m),sb.at[m],rb.at[m],xn)
+    pd=lambda m: W.at[m,:,:,c]
+    def cd(m): return rc(pd(m),pd(m),sd.at[m],rd.at[m],sib)
+    def co(m): return pltpu.make_async_copy(W.at[m], w_out.at[m], so.at[m])
+    def startA(m):
+        @pl.when(c==0)
+        def _(): ca(m,xn).start()
+        @pl.when(c==1)
+        def _(): ca(m,yn).start()
+    def startB(m):
+        @pl.when(c==0)
+        def _(): cb0(m).start()
+        @pl.when(c==1)
+        def _(): cb1(m).start()
+    for m in range(NM): c0(m).start()
+    for m in range(NM):
+        c0(m).wait()
+        own=sh[m,c]; oth=sh_in[m]
+        lo=jnp.where(c==0,own,oth); hi=jnp.where(c==0,oth,own)
+        W[m,z,x,c,:,yc]=jnp.concatenate([lo,hi],axis=-1)
+        for k in range(3): cz(m,k).start()
+    for s in range(NM+3):
+        if s<NM:
+            for k in range(3): cz(s,k).wait()
+            startA(s)
+        if 1<=s<NM+1:
+            m=s-1; ca(m,xn).wait(); startB(m)
+        if 2<=s<NM+2:
+            m=s-2; cb0(m).wait(); cd(m).start()
+        if 3<=s:
+            m=s-3; cd(m).wait(); co(m).start()
+    for m in range(NM): co(m).wait()
+def ag(sh):
+    D=pltpu.SemaphoreType.DMA
+    return pl.pallas_call(ag_kernel,
+      out_shape=jax.ShapeDtypeStruct((NM,4,2,2,80,1280),jnp.bfloat16),
+      in_specs=[pl.BlockSpec(memory_space=pltpu.VMEM)], out_specs=pl.BlockSpec(memory_space=pl.ANY),
+      scratch_shapes=[pltpu.VMEM((NM,4,2,2,80,1280),jnp.bfloat16),pltpu.VMEM((NM,80,320),jnp.bfloat16),
+        D((NM,)),D((NM,)),D((NM,3)),D((NM,3)),D((NM,)),D((NM,)),D((NM,)),D((NM,)),D((NM,)),D((NM,)),D((NM,))],
+      compiler_params=pltpu.CompilerParams(collective_id=0,has_side_effects=True,vmem_limit_bytes=60<<20),
+      name="kag")(sh.reshape(NM,2,80,320))
+
+
+def rs_kernel(G_in, out, G, sG, RD, RB, RA, RZ, F, FX, sD,rD,sB,rB,sA,rA,sZ,rZ,sF,rF):
+    x,y,z,c=ids()
+    sib=dev(x,y,z,1-c); xn=dev(1-x,y,z,c); yn=dev(x,1-y,z,c)
+    zp=[dev(x,y,lax.rem(z+k,4),c) for k in (1,2,3)]
+    bar=pltpu.get_barrier_semaphore()
+    for d in [sib,xn,yn]+zp:
+        pl.semaphore_signal(bar,inc=1,device_id=d,device_id_type=MESH)
+    pl.semaphore_wait(bar,6)
+    def cols(j): return pl.ds(pl.multiple_of(j*640,128),640)
+    def rc(src,dst,s,r,d): return pltpu.make_async_remote_copy(src,dst,s,r,device_id=d,device_id_type=MESH)
+    def cD(m): return rc(G.at[m,:,:,1-c],RD.at[m],sD.at[m],rD.at[m],sib)
+    own2=jnp.where(c==0,x,y)
+    def srcB(m,j,core):
+        return G.at[m,:,j,0,:,cols(1-y)] if core==0 else G.at[m,:,1-x,1,:,cols(j)]
+    def cB(m,t,core):
+        j = 1-own2 if t==0 else own2
+        return rc(srcB(m,j,core),RB.at[m,t],sB.at[m,t],rB.at[m,t],yn if core==0 else xn)
+    def keepB(m,t,core):
+        j = 1-own2 if t==0 else own2
+        return G.at[m,:,j,0,:,cols(y)] if core==0 else G.at[m,:,x,1,:,cols(j)]
+    def cA(m,core): return rc(keepB(m,0,core),RA.at[m],sA.at[m],rA.at[m],xn if core==0 else yn)
+    def cZ(m,k):
+        zt=lax.rem(z+k+1,4)
+        return rc(G.at[m,zt,x,c,:,cols(y)],RZ.at[m,k],sZ.at[m,k],rZ.at[m,k],zp[k])
+    def both(fn):
+        for core in (0,1):
+            @pl.when(c==core)
+            def _(): fn(core)
+    def addD(m):
+        def body(i,_):
+            a=i//2; b=i%2
+            G[m,a,b,c]=G[m,a,b,c]+RD[m,a,b]
+            return 0
+        lax.fori_loop(0,8,body,0)
+    def addB(m,t):
+        def go(core):
+            k=keepB(m,t,core)
+            def body(i,_):
+                k[i]=k[i]+RB[m,t,i]
+                return 0
+            lax.fori_loop(0,4,body,0)
+        both(go)
+    def addA(m):
+        def body(i,_):
+            r=G.at[m,i,x,c,:,cols(y)]
+            r[...]=r[...]+RA[m,i]
+            return 0
+        lax.fori_loop(0,4,body,0)
+    def cG(m): return pltpu.make_async_copy(G_in.at[m], G.at[m], sG.at[m])
+    for m in range(NM): cG(m).start()
+    for s in range(NM+4):
+        if s<NM:
+            cG(s).wait(); cD(s).start()
+        if 1<=s<NM+1:
+            m=s-1; cD(m).wait(); addD(m)
+            both(lambda core: [cB(m,t,core).start() for t in (0,1)])
+        if 2<=s<NM+2:
+            m=s-2
+            both(lambda core: cB(m,0,core).wait()); addB(m,0)
+            both(lambda core: cA(m,core).start())
+            both(lambda core: cB(m,1,core).wait()); addB(m,1)
+        if 3<=s<NM+3:
+            m=s-3
+            cA(m,0).wait(); addA(m)
+            for k in range(3): cZ(m,k).start()
+        if 4<=s:
+            m=s-4
+            for k in range(3): cZ(m,k).wait()
+            f=G[m,z,x,c,:,cols(y)].astype(jnp.float32)
+            for k in range(3): f=f+RZ[m,k].astype(jnp.float32)
+            F[m,0]=f[:,:384]; F[m,1]=f[:,256:]
+    cF=rc(F.at[:,1-c],FX,sF,rF,sib)
+    cF.start(); cF.wait()
+    for m in range(NM):
+        w=F[m,c]; out[m,c]=jnp.where(c==0,w[:,:320],w[:,64:])
+        w=FX[m]; out[m,1-c]=jnp.where(c==0,w[:,:320],w[:,64:])
+def rs(g):
+    D=pltpu.SemaphoreType.DMA; bf=jnp.bfloat16
+    return pl.pallas_call(rs_kernel,
+      out_shape=jax.ShapeDtypeStruct((NM,2,80,320),jnp.float32),
+      in_specs=[pl.BlockSpec(memory_space=pl.ANY)], out_specs=pl.BlockSpec(memory_space=pltpu.VMEM),
+      scratch_shapes=[pltpu.VMEM((NM,4,2,2,80,1280),bf),D((NM,)),pltpu.VMEM((NM,4,2,80,1280),bf),pltpu.VMEM((NM,2,4,80,640),bf),pltpu.VMEM((NM,4,80,640),bf),pltpu.VMEM((NM,3,80,640),bf),
+        pltpu.VMEM((NM,2,80,384),jnp.float32),pltpu.VMEM((NM,80,384),jnp.float32),
+        D((NM,)),D((NM,)),D((NM,2)),D((NM,2)),D((NM,)),D((NM,)),D((NM,3)),D((NM,3)),D,D],
+      compiler_params=pltpu.CompilerParams(collective_id=1,has_side_effects=True,vmem_limit_bytes=60<<20),
+      name="krs")(g.reshape(NM,4,2,2,80,1280)).reshape(NM,160,320)
 
 
 def layer_norm(values, gain_row, bias_row):
@@ -121,7 +286,15 @@
     data_devices = lax.axis_size("dp")
     row_count = latents.shape[0]
     item_count = row_count // LAT
-    inner_b, outer_b = (
+    fast = (data_devices, head_devices) == (8, 4)
+    if fast:
+        whole = ag(jnp.concatenate(
+            [inner_weights[:3], outer_weights[:1].swapaxes(1, 2), inner_weights[3:],
+             outer_weights[1:].swapaxes(1, 2)]).astype(jnp.bfloat16)).reshape(NM, D, D)
+        inner_b = jnp.stack([whole[0], whole[1], whole[2], whole[4]])
+        outer_b = jnp.stack([whole[3].T, whole[5].T])
+    else:
+      inner_b, outer_b = (
         lax.all_gather(
             lax.all_gather(inner_weights.astype(jnp.bfloat16), "dp", axis=1, tiled=True),
             "head", axis=2, tiled=True),
@@ -169,9 +342,15 @@
     norm_back_one = jax.vjp(layer_norm, source, norm_params[0], norm_params[1])[1]
     d_source_norm, grad_gain_one, grad_bias_one = norm_back_one(d_normed)
     latent_grad = (d_resid + d_source_norm).astype(jnp.bfloat16)
-    grad_inner = jnp.concatenate([grad_qkv, grad_up[None]], axis=0)
-    grad_outer = jnp.stack([grad_outproj, grad_down])
-    grad_inner, grad_outer = (
+    if fast:
+        got = rs(jnp.stack([grad_qkv[0], grad_qkv[1], grad_qkv[2], grad_outproj.T, grad_up,
+                            grad_down.T]).astype(jnp.bfloat16))
+        grad_inner = jnp.stack([got[0], got[1], got[2], got[4]])
+        grad_outer = jnp.stack([got[3].T, got[5].T])
+    else:
+      grad_inner = jnp.concatenate([grad_qkv, grad_up[None]], axis=0)
+      grad_outer = jnp.stack([grad_outproj, grad_down])
+      grad_inner, grad_outer = (
         lax.psum_scatter(
             lax.psum_scatter(
                 grad_inner.astype(jnp.bfloat16), "head", scatter_dimension=2, tiled=True

time: 838 us -> 472 us (0.56)
  waiting for transfers between devices: 503 us -> 0 us
  Pallas kernels: 0 us -> 227 us
  local copies, waits for them, and re-layouts: 158 us -> 90.6 us
  between operations: 19.6 us -> 5.6 us
  matrix products: 79.2 us -> 69.8 us
    pallas_call x0 -> x2, Pallas kernels: none -> 227 us  [the longest x1 116 us: rs(): pl.pallas_call(rs_kernel, out_shape=jax.ShapeDtypeStruct((NM, 2, 80, 320)...]
    all_gather x4 -> x0, waiting for transfers between devices: 222 us -> none  [the longest x1 72.3 us: shards(): lax.all_gather(lax.all_gather(inner_weights.astype(jnp.bfloat16), 'dp', a...]
    unnamed x8 -> x0, waiting for transfers between devices: 184 us -> none
    reduce_scatter x2 -> x0, waiting for transfers between devices: 96.1 us -> none  [the longest x1 96 us: shards(): lax.psum_scatter(grad_inner.astype(jnp.bfloat16), 'head', scatter_dimensi...]
    unnamed x88 -> x89, local copies, waits for them, and re-layouts: 50.4 us -> 5.58 us
    all_gather x2 -> x0, local copies, waits for them, and re-layouts: 16.3 us -> none  [the longest x1 8.87 us: shards(): lax.all_gather(inner_weights.astype(jnp.bfloat16), 'dp', axis=1, tiled=True)]
    reduce_scatter x2 -> x0, local copies, waits for them, and re-layouts: 14.5 us -> none  [the longest x1 7.83 us: shards(): lax.psum_scatter(grad_inner.astype(jnp.bfloat16), 'head', scatter_dimensi...]
    another operation x6 -> x3, local copies, waits for them, and re-layouts: 20.3 us -> 11.8 us  [split_heads(): matrix.reshape(item_count, matrix.shape[0] // item_count, head_count, mat...]
  transfers between devices with their start and end apart: 7 -> 0, of which waited for: 6 -> 0; matrix products, arithmetic and copies ran while one was open for 15% -> 0% of each run, Pallas kernels for 0% -> 0%
where the time goes in v2:
time: 472 us; the launch traced here: 463 us
  Pallas kernels  227 us (48%)
  local copies, waits for them, and re-layouts  90.6 us (19%)
  matrix products  69.8 us (15%)
  blocking collectives  39.9 us (8%)
  other arithmetic  29.3 us (6%)
  between operations  5.6 us (1%)
    pallas_call x1, Pallas kernels, rs(): pl.pallas_call(rs_kernel, out_shape=jax.ShapeDtypeStruct((NM, 2, 80, 320)...  116 us
    pallas_call x1, Pallas kernels, ag(): pl.pallas_call(ag_kernel, out_shape=jax.ShapeDtypeStruct((NM, 4, 2, 2, 80...  111 us
    psum x1, blocking collectives, shards(): lax.psum((norm_part, local_squares), ('dp', 'head'))  39.9 us
    another operation x7, local copies, waits for them, and re-layouts, attend_back(): jnp.stack([d_query.reshape(flat_shape), d_key.reshape(flat_shape), d_valu...  27 us
    slice x3, local copies, waits for them, and re-layouts, shards(): inner_b = jnp.stack([whole[0], whole[1], whole[2], whole[4]])  14.9 us
    slice x1, local copies, waits for them, and re-layouts, shards(): outer_b = jnp.stack([whole[3].T, whole[5].T])  12.8 us
    another operation x3, local copies, waits for them, and re-layouts, split_heads(): matrix.reshape(item_count, matrix.shape[0] // item_count, head_count, mat...  11.8 us

profile of v2, /device:TPU:0, one launch (start us, length us, event | category | flops | bytes accessed | tf_op | source)
XLA Modules:
  0.0 462.6 jit_solution(2180048473560851173)
XLA Ops:
  6.3 111.1 %kag.1 = bf16[6,4,2,2,80,1280]{5,4,3,2,1,0:T(8,128)(2,1)} custom-call(bf16[6,2,80,320]{3,2,1,0:T(8,128)(2,1)} %pad_maximum_fusion.9.sh), custom_call_target="tpu_custom_call" | custom-call | tf_op jit(solution)/shard_map/kag/pallas_call | solution.py:90
  117.5 12.8 %fusion.63 = (bf16[1,4,2,2,80,1280]{5,4,3,2,1,0:T(8,128)(2,1)}, bf16[1,4,2,2,80,1280]{5,4,3,2,1,0:T(8,128)(2,1)}, bf16[1,4,2,2,80,1280]{5,4,3,2,1,0:T(8,128)(2,1...) fusion(bf16[6,4,2,2,80,1280]{5,4,3,2,1,0:T(8,128)(2,1)} %kag.1), kind=kLoop, calls=%fused_computation.132 | loop fusion | bytes 39321600 | tf_op jit(solution)/shard_map/slice | solution.py:295
  130.3 5.6 %copy.53 = bf16[1,1280,1280]{1,2,0:T(8,128)(2,1)} copy(bf16[1,1280,1280]{2,1,0:T(8,128)(2,1)} %bitcast.103) | data formatting | bytes 6553600 | tf_op jit(solution)/shard_map/slice | solution.py:294
  139.4 5.8 %copy.51 = bf16[1,1280,1280]{1,2,0:T(8,128)(2,1)} copy(bf16[1,1280,1280]{2,1,0:T(8,128)(2,1)} %bitcast.101) | data formatting | bytes 6553600 | tf_op jit(solution)/shard_map/slice | solution.py:294
  145.2 8.4 %fusion.5 = bf16[3,512,1280]{1,2,0:T(8,128)(2,1)S(1)} fusion(bf16[1,1280,1280]{1,2,0:T(8,128)(2,1)} %copy.53, bf16[1,1280,1280]{1,2,0:T(8,128)(2,1)} %copy.52, bf16[1,1280,1280]{1,2,0:T(8,128)(2,1)} %copy.51, bf16[512,1280]{1,0:T(8,128)(2,1)S(1)} %copy-done.2, f32[1280]{0:T(1024)S(1)} %get-tuple-element.24, f32[1280]{0:T(1024)S(1)} %get-tuple-element.25, ...), kind=kOutput, calls=%fused_computation.23 | convolution fusion | flops 5048893440 | bytes 15087616 | tf_op jit(solution)/shard_map/rd,tdc->trc/dot_general | solution.py:313
  158.8 4.4 reshape_squeeze.14
  163.2 4.2 reshape_squeeze.12
  178.0 7.6 %multiply_convert_fusion.3 = (bf16[512,1280]{1,0:T(8,128)(2,1)S(1)}, f32[512,1280]{1,0:T(8,128)S(1)}, f32[512,1280]{1,0:T(8,128)S(1)}) fusion(bf16[1280,1280]{1,0:T(8,128)(2,1)S(1)} %bitcast.110, f32[512,1280]{1,0:T(8,128)S(1)} %get-tuple-element.65, f32[1280]{0:T(1024)S(1)} %get-tuple-element.26, f32[1280]{0:T(1024)S(1)} %get-tuple-element.23, ...), kind=kOutput, calls=%fused_computation.46 | convolution fusion | flops 1723596800 | bytes 12466176 | tf_op jit(solution)/shard_map/dot_general | solution.py:319
  203.8 5.3 %fusion.6 = bf16[1,4,2,2,80,1280]{5,4,3,2,1,0:T(8,128)(2,1)} fusion(bf16[4,2,2,80,512]{4,3,2,1,0:T(8,128)(2,1)} %bitcast.130, bf16[512,1280]{0,1:T(8,128)(2,1)} %bitcast.129), kind=kOutput, calls=%fused_computation.24 | convolution fusion | flops 1679360000 | bytes 5898240 | tf_op jit(solution)/shard_map/rc,rd->cd/dot_general | solution.py:333
  209.1 4.9 %reshape.200 = bf16[2,256,8,160]{3,2,1,0:T(8,128)(2,1)} reshape(bf16[512,1280]{1,0:T(8,128)(2,1)} %convolution_convert_fusion.5) | data formatting | bytes 2621440 | tf_op jit(solution)/shard_map/reshape | solution.py:198
  213.9 4.4 copy.61
  218.4 4.9 %fusion.26 = bf16[2,256,8,160]{1,3,2,0:T(8,128)(2,1)} fusion(bf16[2,256,8,160]{1,3,2,0:T(8,128)(2,1)} %copy.61, f32[2,8,256,256]{2,3,1,0:T(8,128)} %copy-done, f32[2,8,256]{2,1,0:T(8,128)S(1)} %log_add_fusion, pred[2,256]{1,0:T(4,128)(4,1)S(1)} %iota_compare_fusion), kind=kOutput, calls=%fused_computation.67 | convolution fusion | flops 340393984 | bytes 6832640 | tf_op jit(solution)/shard_map/ihqk,iqhd->ikhd/dot_general | solution.py:239
  223.3 4.3 copy.89
  227.6 4.6 reshape.199
  232.2 4.8 %multiply_reduce_fusion = (f32[2,8,256]{2,1,0:T(8,128)S(1)}, f32[2,8,256,256]{2,3,1,0:T(8,128)S(1)}) fusion(f32[2,8,256,256]{2,3,1,0:T(8,128)} %copy-done, f32[2,8,256]{2,1,0:T(8,128)S(1)} %log_add_fusion, pred[2,256]{1,0:T(4,128)(4,1)S(1)} %iota_compare_fusion, bf16[2,256,8,160]{1,3,2,0:T(8,128)(2,1)} %copy.61, bf16[2,256,8,160]{1,0,3,2:T(2,128)(2,1)} %reshape_squeeze.12), kind=kOutput, calls=%fused_computation.7 | convolution fusion | flops 340783104 | bytes 11043328 | tf_op jit(solution)/shard_map/iqhd,ikhd->ihqk/dot_general | solution.py:240
  241.9 4.3 copy.87
  246.2 4.6 reshape.197
  250.8 4.3 copy.88
  255.1 4.8 %reshape.198 = bf16[1,512,1280]{2,1,0:T(8,128)(2,1)} reshape(bf16[2,256,8,160]{3,2,1,0:T(8,128)(2,1)} %copy.88) | data formatting | bytes 2621440 | tf_op jit(solution)/shard_map/stack;reshape | solution.py:256
  267.4 5.4 %fusion.16 = (f32[512]{0:T(512)S(1)}, f32[512,1280]{1,0:T(8,128)S(1)}) fusion(bf16[512,1280]{1,0:T(8,128)(2,1)S(1)} %copy-done.3, f32[1280]{0:T(1024)S(1)} %get-tuple-element.25, f32[512]{0:T(512)S(1)} %broadcast_multiply_fusion.2, bf16[3,512,1280]{2,1,0:T(8,128)(2,1)S(1)} %constant_dynamic-update-slice_fusion, bf16[1,1280,1280]{1,2,0:T(8,128)(2,1)S(1)} %copy-done.22, ...), kind=kOutput, calls=%fused_computation.37 | convolution fusion | flops 5046271488 | bytes 17703936 | tf_op jit(solution)/shard_map/trc,tdc->rd/dot_general | solution.py:341
  276.5 6.0 %convolution_convert_fusion = bf16[3,1280,1280]{1,2,0:T(8,128)(2,1)S(1)} fusion(bf16[3,512,1280]{2,1,0:T(8,128)(2,1)S(1)} %copy-done.36, bf16[512,1280]{1,0:T(8,128)(2,1)S(1)} %copy-done.3, f32[1280]{0:T(1024)S(1)} %get-tuple-element.24, f32[1280]{0:T(1024)S(1)} %get-tuple-element.25, f32[512]{0:T(512)S(1)} %fusion.46, f32[512]{0:T(512)S(1)} %broadcast_multiply_fusion.2), kind=kOutput, calls=%fused_computation.1 | convolution fusion | flops 5042012160 | bytes 15087616 | tf_op jit(solution)/shard_map/rd,trc->tdc/dot_general | solution.py:340
  282.5 8.8 %pad_maximum_fusion.G_in = bf16[6,4,2,2,80,1280]{5,4,3,2,1,0:T(8,128)(2,1)} fusion(bf16[1,4,2,2,80,1280]{5,4,3,2,1,0:T(8,128)(2,1)S(1)} %bitcast.114, bf16[1,4,2,2,80,1280]{5,4,3,2,1,0:T(8,128)(2,1)S(1)} %bitcast.107, bf16[1,4,2,2,80,1280]{5,4,3,2,1,0:T(8,128)(2,1)S(1)} %copy-done.18, bf16[3,4,2,2,80,1280]{5,4,3,2,1,0:T(8,128)(2,1)S(1)} %bitcast.104), kind=kLoop, calls=%fused_computation | loop fusion | flops 29491200 | bytes 39321600 | tf_op jit(solution)/shard_map/stack | solution.py:346
  291.3 116.2 %krs.1 = f32[6,2,80,320]{3,2,1,0:T(8,128)} custom-call(bf16[6,4,2,2,80,1280]{5,4,3,2,1,0:T(8,128)(2,1)} %pad_maximum_fusion.G_in), custom_call_target="tpu_custom_call" | custom-call | tf_op jit(solution)/shard_map/krs/pallas_call | solution.py:177
  412.2 39.9 %all-reduce = (f32[]{:T(128)}, f32[4,1280]{1,0:T(4,128)S(1)}) all-reduce(f32[]{:T(128)S(6)} %add.140, f32[4,1280]{1,0:T(4,128)S(1)} %pad_maximum_fusion.11), channel_id=1, replica_groups=mesh['dp'=8,'head'=4] {'dp','head'}, use_global_device_ids=true, to_apply=%region_13.14 | all-reduce | flops 5121 | bytes 40968 | tf_op jit(solution)/shard_map/psum | solution.py:365
  (148 shorter events, 69.5 us)
Async XLA Ops:
  0.7 4.3 copy-start.37
  0.7 4.4 copy-start.25
  0.7 4.5 copy-start.14
  139.4 5.8 %copy-start.2 = (bf16[512,1280]{1,0:T(8,128)(2,1)S(1)}, bf16[512,1280]{1,0:T(8,128)(2,1)}, u32[]{:S(2)}) copy-start(bf16[512,1280]{1,0:T(8,128)(2,1)} %param.15) | copy-start | bytes 3932164
  158.8 8.7 %copy-start.4 = (bf16[2,256,8,160]{1,0,3,2:T(2,128)(2,1)}, bf16[2,256,8,160]{1,0,3,2:T(2,128)(2,1)S(1)}, u32[]{:S(2)}) copy-start(bf16[2,256,8,160]{1,0,3,2:T(2,128)(2,1)S(1)} %reshape_squeeze.13) | copy-start | bytes 3932164
  170.0 3.5 copy-start
  178.0 7.6 %copy-start.8 = (bf16[512,1280]{1,0:T(8,128)(2,1)S(1)}, bf16[512,1280]{1,0:T(8,128)(2,1)}, u32[]{:S(2)}) copy-start(bf16[512,1280]{1,0:T(8,128)(2,1)} %param.17) | copy-start | bytes 3932164
  178.0 7.6 %copy-start.21 = (bf16[1,4,2,2,80,1280]{5,4,3,2,1,0:T(8,128)(2,1)S(1)}, bf16[1,4,2,2,80,1280]{5,4,3,2,1,0:T(8,128)(2,1)}, u32[]{:S(2)}) copy-start(bf16[1,4,2,2,80,1280]{5,4,3,2,1,0:T(8,128)(2,1)} %get-tuple-element.45) | copy-start | bytes 9830404
  198.2 3.0 copy-start.13
  232.2 4.8 %copy-start.1 = (f32[2,8,256,256]{2,3,1,0:T(8,128)S(1)}, f32[2,8,256,256]{2,3,1,0:T(8,128)}, u32[]{:S(2)}) copy-start(f32[2,8,256,256]{2,3,1,0:T(8,128)} %copy-done) | copy-start | bytes 12582916
  259.9 3.8 copy-start.11
  259.9 5.6 %copy-start.23 = (bf16[1,1280,1280]{1,2,0:T(8,128)(2,1)S(1)}, bf16[1,1280,1280]{1,2,0:T(8,128)(2,1)}, u32[]{:S(2)}) copy-start(bf16[1,1280,1280]{1,2,0:T(8,128)(2,1)} %copy.52) | copy-start | bytes 9830404
  259.9 5.6 %copy-start.24 = (bf16[1,1280,1280]{1,2,0:T(8,128)(2,1)S(1)}, bf16[1,1280,1280]{1,2,0:T(8,128)(2,1)}, u32[]{:S(2)}) copy-start(bf16[1,1280,1280]{1,2,0:T(8,128)(2,1)} %copy.51) | copy-start | bytes 9830404
  267.4 5.4 %copy-start.35 = (bf16[3,512,1280]{2,1,0:T(8,128)(2,1)}, bf16[3,512,1280]{2,1,0:T(8,128)(2,1)S(1)}, u32[]{:S(2)}) copy-start(bf16[3,512,1280]{2,1,0:T(8,128)(2,1)S(1)} %constant_dynamic-update-slice_fusion) | copy-start | bytes 11796484
  276.5 6.0 %copy-start.17 = (bf16[1280,1280]{1,0:T(8,128)(2,1)S(1)}, bf16[1280,1280]{1,0:T(8,128)(2,1)}, u32[]{:S(2)}) copy-start(bf16[1280,1280]{1,0:T(8,128)(2,1)} %convolution_convert_fusion.2) | copy-start | bytes 9830404
  276.5 6.0 %copy-start.18 = (bf16[1,4,2,2,80,1280]{5,4,3,2,1,0:T(8,128)(2,1)S(1)}, bf16[1,4,2,2,80,1280]{5,4,3,2,1,0:T(8,128)(2,1)}, u32[]{:S(2)}) copy-start(bf16[1,4,2,2,80,1280]{5,4,3,2,1,0:T(8,128)(2,1)} %fusion.6) | copy-start | bytes 9830404
  407.5 46.5 %copy-start.38 = (f32[4,1280]{1,0:T(4,128)S(1)}, f32[4,1280]{1,0:T(4,128)}, u32[]{:S(2)}) copy-start(f32[4,1280]{1,0:T(4,128)} %param.20) | copy-start | bytes 61444
  407.6 46.5 %copy-start.39 = (f32[4,1280]{1,0:T(4,128)S(1)}, f32[4,1280]{1,0:T(4,128)}, u32[]{:S(2)}) copy-start(f32[4,1280]{1,0:T(4,128)} %param.28) | copy-start | bytes 61444
  407.6 46.5 %copy-start.40 = (f32[4,1280]{1,0:T(4,128)S(1)}, f32[4,1280]{1,0:T(4,128)}, u32[]{:S(2)}) copy-start(f32[4,1280]{1,0:T(4,128)} %param.27) | copy-start | bytes 61444
  407.6 47.8 %copy-start.26 = (f32[2,320,160]{1,2,0:T(8,128)S(1)}, f32[2,320,160]{1,2,0:T(8,128)}, u32[]{:S(2)}) copy-start(f32[2,320,160]{1,2,0:T(8,128)} %param.19) | copy-start | bytes 1228804
  407.6 47.7 %copy-start.32 = (f32[2,320,160]{1,2,0:T(8,128)S(1)}, f32[2,320,160]{1,2,0:T(8,128)}, u32[]{:S(2)}) copy-start(f32[2,320,160]{1,2,0:T(8,128)} %param.25) | copy-start | bytes 1228804
  407.6 47.7 %copy-start.33 = (f32[2,320,160]{1,2,0:T(8,128)S(1)}, f32[2,320,160]{1,2,0:T(8,128)}, u32[]{:S(2)}) copy-start(f32[2,320,160]{1,2,0:T(8,128)} %param.24) | copy-start | bytes 1228804
  407.6 47.7 %copy-start.41 = (f32[2]{0:T(128)S(1)}, f32[2]{0:T(128)}, u32[]{:S(2)}) copy-start(f32[2]{0:T(128)} %constant.127.clone) | copy-start | bytes 28
  409.3 47.4 %copy-start.34 = (f32[2,320,160]{1,2,0:T(8,128)S(1)}, f32[2,320,160]{1,2,0:T(8,128)}, u32[]{:S(2)}) copy-start(f32[2,320,160]{1,2,0:T(8,128)} %param.26) | copy-start | bytes 1228804
  (19 other events, 40.1 us)

commit v3 on v1

--- a/solution.py
+++ b/solution.py
@@ -1,6 +1,8 @@
 import jax
 import jax.numpy as jnp
 from jax import lax
+from jax.experimental import pallas as pl
+from jax.experimental.pallas import tpu as pltpu
 from jax.sharding import PartitionSpec as P
 
 HEADS = 8
@@ -17,6 +19,478 @@
 DECAY_RATE = 0.1
 NORM_RATE = 0.3
 SMOOTH_RATE = 0.9
+
+
+NM = 6
+MESH = pl.DeviceIdType.MESH
+NN = (((1,), (0,)), ((), ()))
+NT = (((1,), (1,)), ((), ()))
+TN = (((0,), (0,)), ((), ()))
+ROWS = 512
+CH = 64
+SLOT = {5: 6, 4: 5, 3: 4, 0: 3, 1: 0, 2: 1}
+RD_SLOTS = 2
+
+
+def ids():
+    d = lax.axis_index("dp")
+    h = lax.axis_index("head")
+    return d % 2, h // 2, d // 2, h % 2
+
+
+def dev(x, y, z, c):
+    return (z * 2 + x, y * 2 + c)
+
+
+def dg(a, b, dims):
+    return lax.dot_general(a, b, dims, preferred_element_type=jnp.float32)
+
+
+def block_kernel(
+    sh, lat_in, cot_in, live, norms,
+    bo_out, lg_out, gout, nout,
+    W, sh_in, lat, cot, n1, q, k, v, probs, att, resid, n2, act, gp, T,
+    RD, RB, RA, RZ, F, FX, NG, NX, SQ, SX,
+    s0, r0, sz, rz, sa, ra, sb, rb, sd, rd,
+    sD, rD, sB, rB, sA, rA, sZ, rZ, sF, rF, sN, rN, sS, rS, lsem, free,
+):
+    bf, f32 = jnp.bfloat16, jnp.float32
+    x, y, z, c = ids()
+    sib, xn, yn = dev(x, y, z, 1 - c), dev(1 - x, y, z, c), dev(x, 1 - y, z, c)
+    zp = [dev(x, y, lax.rem(z + j, 4), c) for j in (1, 2, 3)]
+
+    c_lat = pltpu.make_async_copy(lat_in, lat, lsem.at[0])
+    c_cot = pltpu.make_async_copy(cot_in, cot, lsem.at[1])
+    c_lat.start()
+    c_cot.start()
+    bar = pltpu.get_barrier_semaphore()
+    for d in [sib, xn, yn] + zp:
+        pl.semaphore_signal(bar, inc=1, device_id=d, device_id_type=MESH)
+    pl.semaphore_wait(bar, 6)
+
+    def cols(j):
+        return pl.ds(pl.multiple_of(j * 640, 128), 640)
+
+    def rc(src, dst, s, r, d):
+        return pltpu.make_async_remote_copy(src, dst, s, r, device_id=d, device_id_type=MESH)
+
+    def both(fn):
+        for core in (0, 1):
+            @pl.when(c == core)
+            def _():
+                fn(core)
+
+    def g_pair(m):
+        return rc(sh.at[m, 1 - c], sh_in.at[m], s0.at[m], r0.at[m], sib)
+
+    def g_z(m, j):
+        u = W.at[m, z, x, c, :, cols(y)]
+        return rc(u, u, sz.at[m, j], rz.at[m, j], zp[j])
+
+    def g_a(m, core):
+        u = W.at[m, :, x, c, :, cols(y)]
+        return rc(u, u, sa.at[m], ra.at[m], xn if core == 0 else yn)
+
+    def g_b(m, core):
+        u = W.at[m, :, :, 0, :, cols(y)] if core == 0 else W.at[m, :, x, 1, :, :]
+        return rc(u, u, sb.at[m], rb.at[m], yn if core == 0 else xn)
+
+    def g_d(m):
+        u = W.at[m, :, :, c]
+        return rc(u, u, sd.at[m], rd.at[m], sib)
+
+    def g_first(m):
+        g_pair(m).wait()
+        own, oth = sh[m, c], sh_in[m]
+        W[m, z, x, c, :, cols(y)] = jnp.concatenate(
+            [jnp.where(c == 0, own, oth), jnp.where(c == 0, oth, own)], axis=-1
+        )
+        for j in range(3):
+            g_z(m, j).start()
+
+    def g_step(s):
+        if s + 1 < NM:
+            g_first(s + 1)
+        if s < NM:
+            for j in range(3):
+                g_z(s, j).wait()
+            both(lambda core: g_a(s, core).start())
+        if 0 <= s - 1 < NM:
+            g_a(s - 1, 0).wait()
+            both(lambda core: g_b(s - 1, core).start())
+        if 0 <= s - 2 < NM:
+            g_b(s - 2, 0).wait()
+            g_d(s - 2).start()
+
+    own2 = jnp.where(c == 0, x, y)
+
+    def r_d(m):
+        return rc(W.at[SLOT[m], :, :, 1 - c], RD.at[ORD[m] % RD_SLOTS], sD.at[m], rD.at[m], sib)
+
+    def half(t):
+        return 1 - own2 if t == 0 else own2
+
+    def r_b(m, t, core):
+        g = W.at[SLOT[m]]
+        src = g.at[:, half(t), 0, :, cols(1 - y)] if core == 0 else g.at[:, 1 - x, 1, :, cols(half(t))]
+        return rc(src, RB.at[m, t], sB.at[m, t], rB.at[m, t], yn if core == 0 else xn)
+
+    def keep_b(m, t, core):
+        g = W.at[SLOT[m]]
+        return g.at[:, half(t), 0, :, cols(y)] if core == 0 else g.at[:, x, 1, :, cols(half(t))]
+
+    def r_a(m, core):
+        return rc(keep_b(m, 0, core), RA.at[m], sA.at[m], rA.at[m], xn if core == 0 else yn)
+
+    def r_z(m, j):
+        zt = lax.rem(z + j + 1, 4)
+        return rc(W.at[SLOT[m], zt, x, c, :, cols(y)], RZ.at[m, j], sZ.at[m, j], rZ.at[m, j], zp[j])
+
+    def r_f(m):
+        return rc(F.at[m], FX.at[m], sF.at[m], rF.at[m], sib)
+
+    def st_d(m):
+        if ORD[m] >= RD_SLOTS:
+            pl.semaphore_wait(free, 1)
+        r_d(m).start()
+
+    def st_b(m):
+        r_d(m).wait()
+
+        def body(i, _):
+            a, b = i // 2, i % 2
+            W[SLOT[m], a, b, c] = W[SLOT[m], a, b, c] + RD[ORD[m] % RD_SLOTS, a, b]
+            return 0
+
+        lax.fori_loop(0, 8, body, 0)
+        if ORD[m] + RD_SLOTS < NM:
+            pl.semaphore_signal(free, inc=1, device_id=sib, device_id_type=MESH)
+        both(lambda core: [r_b(m, t, core).start() for t in (0, 1)])
+
+    def add_b(m, t):
+        def go(core):
+            kept = keep_b(m, t, core)
+
+            def body(i, _):
+                kept[i] = kept[i] + RB[m, t, i]
+                return 0
+
+            lax.fori_loop(0, 4, body, 0)
+
+        both(go)
+
+    def st_a(m):
+        both(lambda core: r_b(m, 0, core).wait())
+        add_b(m, 0)
+        both(lambda core: r_a(m, core).start())
+        both(lambda core: r_b(m, 1, core).wait())
+        add_b(m, 1)
+
+    def st_z(m):
+        r_a(m, 0).wait()
+
+        def body(i, _):
+            r = W.at[SLOT[m], i, x, c, :, cols(y)]
+            r[...] = r[...] + RA[m, i]
+            return 0
+
+        lax.fori_loop(0, 4, body, 0)
+        for j in range(3):
+            r_z(m, j).start()
+
+    def st_f(m):
+        for j in range(3):
+            r_z(m, j).wait()
+        f = W[SLOT[m], z, x, c, :, cols(y)].astype(f32)
+        for j in range(3):
+            f = f + RZ[m, j].astype(f32)
+        F[m] = jnp.where(c == 0, f[:, 256:], f[:, :384])
+        gout[m, c] = jnp.where(c == 0, f[:, :320], f[:, 320:])
+        r_f(m).start()
+        ff = f * f
+        ff = ff.reshape(10, 8, 640).sum(0)
+        SQ[0] += ff[:, :128] + ff[:, 128:256] + ff[:, 256:384] + ff[:, 384:512] + ff[:, 512:]
+
+    def mat(m):
+        return W[m].reshape(D, D)
+
+    def chunks(fn, init=0):
+        return lax.fori_loop(
+            0, ROWS // CH, lambda i, a: fn(pl.ds(pl.multiple_of(i * CH, CH), CH), a), init)
+
+    def stats(vals):
+        centre = vals - jnp.mean(vals, axis=-1, keepdims=True)
+        r = lax.rsqrt(jnp.mean(centre * centre, axis=-1, keepdims=True) + NORM_EPS)
+        return centre * r, r
+
+    def ln_to(src, gi, dst):
+        def body(r, a):
+            xhat, _ = stats(src[r, :].astype(f32))
+            dst[r, :] = (xhat * norms[gi:gi + 1, :] + norms[gi + 1:gi + 2, :]).astype(bf)
+            return a
+
+        chunks(body)
+
+    def ln_back(src, gi, err, emit):
+        def body(r, acc):
+            xhat, inv = stats(src[r, :].astype(f32))
+            e = err[r, :]
+            eg = e * norms[gi:gi + 1, :]
+            back = inv * (eg - jnp.mean(eg, axis=-1, keepdims=True)
+                          - xhat * jnp.mean(eg * xhat, axis=-1, keepdims=True))
+            emit(r, back)
+            return (acc[0] + (e * xhat).reshape(CH // 8, 8, D).sum(0),
+                    acc[1] + e.reshape(CH // 8, 8, D).sum(0))
+
+        zero = jnp.zeros((8, D), f32)
+        a, b = chunks(body, (zero, zero))
+        NG[0, gi:gi + 1, :] = a.sum(0, keepdims=True)
+        NG[0, gi + 1:gi + 2, :] = b.sum(0, keepdims=True)
+
+    scale = HS ** (-0.5)
+    lane = lax.broadcasted_iota(jnp.int32, (1, 256), 1)
+    lane1 = lax.broadcasted_iota(jnp.int32, (1, 128), 1)
+
+    def head_mask(hh):
+        return jnp.where((lane >= 32 * hh) & (lane < 32 * hh + HS), 1.0, 0.0).astype(bf)
+
+    def join(o, dst, rows, g):
+        parts = [o[0][:, :128]]
+        for hh in (1, 2, 3):
+            parts.append(jnp.where(lane1 < 32 * hh, o[hh - 1][:, 128:], o[hh][:, :128]))
+        parts.append(o[3][:, 128:])
+        for j in range(5):
+            dst[rows, pl.ds(pl.multiple_of(g * 640 + 128 * j, 128), 128)] = parts[j].astype(bf)
+
+    h_first = (y * 2 + c) * 2
+
+    def attn(i, g):
+        rows = pl.ds(pl.multiple_of(i * LAT, LAT), LAT)
+        count = live[h_first + i]
+        outs = []
+        for hh in range(4):
+            win = pl.ds(pl.multiple_of(g * 640 + 128 * hh, 128), 256)
+            s = dg(q[rows, win] * head_mask(hh), k[rows, win], NT) * scale
+            s = jnp.where(lane < count, s, MASKED)
+            e = jnp.exp(s - jnp.max(s, axis=-1, keepdims=True))
+            p = (e * (1.0 / jnp.sum(e, axis=-1, keepdims=True))).astype(bf)
+            probs[i * 8 + g * 4 + hh] = p
+            outs.append(dg(p, v[rows, win], NN))
+        join(outs, att, rows, g)
+
+    def attn_back(i, g, do, dq, dk, dv):
+        rows = pl.ds(pl.multiple_of(i * LAT, LAT), LAT)
+        oq, ok, ov = [], [], []
+        for hh in range(4):
+            win = pl.ds(pl.multiple_of(g * 640 + 128 * hh, 128), 256)
+            p = probs[i * 8 + g * 4 + hh]
+            dow = do[rows, win]
+            ov.append(dg(p, dow, TN))
+            dp = dg(dow * head_mask(hh), v[rows, win], NT)
+            pf = p.astype(f32)
+            ds = (pf * (dp - jnp.sum(pf * dp, axis=-1, keepdims=True))).astype(bf)
+            oq.append(dg(ds, k[rows, win], NN) * scale)
+            ok.append(dg(ds, q[rows, win], TN) * scale)
+        join(oq, dq, rows, g)
+        join(ok, dk, rows, g)
+        join(ov, dv, rows, g)
+
+    for m in range(NM):
+        g_pair(m).start()
+    g_first(0)
+    c_lat.wait()
+    ln_to(lat, 0, n1)
+    g_step(0)
+    g_step(1)
+    g_step(2)
+    g_step(3)
+    g_d(0).wait()
+    q[...] = dg(n1[...], mat(0), NN).astype(bf)
+    g_step(4)
+    g_d(1).wait()
+    k[...] = dg(n1[...], mat(1), NN).astype(bf)
+    g_step(5)
+    g_d(2).wait()
+    v[...] = dg(n1[...], mat(2), NN).astype(bf)
+    lax.fori_loop(0, 2, lambda i, a: (attn(i, 0), 0)[1], 0)
+    g_step(6)
+    lax.fori_loop(0, 2, lambda i, a: (attn(i, 1), 0)[1], 0)
+    g_d(3).wait()
+    T[...] = dg(att[...], mat(3), NT)
+
+    def add_lat(r, a):
+        resid[r, :] = T[r, :] + lat[r, :].astype(f32)
+        return a
+
+    chunks(add_lat)
+    ln_to(resid, 2, n2)
+    g_step(7)
+    g_d(4).wait()
+    T[...] = dg(n2[...], mat(4), NN)
+
+    def gelu(r, a):
+        p = T[r, :]
+        cdf = 0.5 * (1.0 + lax.erf(p * (0.5 ** 0.5)))
+        act[r, :] = (p * cdf).astype(bf)
+        gp[r, :] = (cdf + p * (jnp.exp(-0.5 * p * p) * 0.3989422804014327)).astype(bf)
+        return a
+
+    chunks(gelu)
+    c_cot.wait()
+    W[SLOT[5]] = dg(cot[...], act[...], TN).astype(bf).reshape(4, 2, 2, 80, D)
+    st_d(5)
+    g_d(5).wait()
+    T[...] = dg(cot[...], mat(5), NN)
+
+    def to_pre(r, a):
+        gp[r, :] = (T[r, :] * gp[r, :].astype(f32)).astype(bf)
+        return a
+
+    chunks(to_pre)
+    T[...] = dg(act[...], mat(5), NT)
+
+    def to_bo(r, a):
+        act[r, :] = (T[r, :] + resid[r, :]).astype(bf)
+        return a
+
+    chunks(to_bo)
+    c_bo = pltpu.make_async_copy(act, bo_out, lsem.at[2])
+    c_bo.start()
+    st_b(5)
+    W[SLOT[4]] = dg(n2[...], gp[...], TN).astype(bf).reshape(4, 2, 2, 80, D)
+    st_d(4)
+    T[...] = dg(gp[...], mat(4), NT)
+
+    def emit_two(r, back):
+        d = cot[r, :].astype(f32) + back
+        resid[r, :] = d
+        n2[r, :] = d.astype(bf)
+
+    ln_back(resid, 2, T, emit_two)
+    st_b(4)
+    W[SLOT[3]] = dg(n2[...], att[...], TN).astype(bf).reshape(4, 2, 2, 80, D)
+    st_d(3)
+    c_bo.wait()
+    act[...] = dg(n2[...], mat(3), NN).astype(bf)
+    st_b(3)
+    lax.fori_loop(0, 2, lambda i, a: (attn_back(i, 0, act, cot, gp, att), 0)[1], 0)
+    st_a(5)
+    lax.fori_loop(0, 2, lambda i, a: (attn_back(i, 1, act, cot, gp, att), 0)[1], 0)
+    W[SLOT[0]] = dg(n1[...], cot[...], TN).astype(bf).reshape(4, 2, 2, 80, D)
+    st_d(0)
+    T[...] = dg(cot[...], mat(0), NT)
+    st_a(4)
+    st_z(5)
+    st_b(0)
+    W[SLOT[1]] = dg(n1[...], gp[...], TN).astype(bf).reshape(4, 2, 2, 80, D)
+    st_d(1)
+    T[...] += dg(gp[...], mat(1), NT)
+    st_b(1)
+    W[SLOT[2]] = dg(n1[...], att[...], TN).astype(bf).reshape(4, 2, 2, 80, D)
+    st_d(2)
+    T[...] += dg(att[...], mat(2), NT)
+    st_a(3)
+    st_b(2)
+
+    def emit_one(r, back):
+        n2[r, :] = (resid[r, :] + back).astype(bf)
+
+    ln_back(lat, 0, T, emit_one)
+    c_lg = pltpu.make_async_copy(n2, lg_out, lsem.at[3])
+    c_lg.start()
+
+    def n_swap(t, d):
+        cp = rc(NG.at[0], NX.at[t], sN.at[t], rN.at[t], d)
+        return cp
+
+    SQ[0] = jnp.zeros((8, 128), f32)
+    n_swap(0, sib).start()
+    st_z(4)
+    st_f(5)
+    n_swap(0, sib).wait()
+    NG[0] = NG[0] + NX[0]
+    n_swap(1, xn).start()
+    st_a(0)
+    st_z(3)
+    st_f(4)
+    n_swap(1, xn).wait()
+    NG[0] = NG[0] + NX[1]
+    n_swap(2, yn).start()
+    st_a(1)
+    st_z(0)
+    st_f(3)
+    n_swap(2, yn).wait()
+    NG[0] = NG[0] + NX[2]
+    for j in range(3):
+        n_swap(3 + j, zp[j]).start()
+    st_a(2)
+    st_z(1)
+    st_f(0)
+    st_z(2)
+    st_f(1)
+    st_f(2)
+    for j in range(3):
+        n_swap(3 + j, zp[j]).wait()
+    NG[0] = NG[0] + NX[3] + NX[4] + NX[5]
+
+    def s_swap(t, d):
+        return rc(SQ.at[0], SX.at[t], sS.at[t], rS.at[t], d)
+
+    for t, d in enumerate((sib, xn, yn)):
+        s_swap(t, d).start()
+        s_swap(t, d).wait()
+        SQ[0] = SQ[0] + SX[t]
+    for j in range(3):
+        s_swap(3 + j, zp[j]).start()
+    for m in range(NM):
+        r_f(m).wait()
+        w = FX[m]
+        gout[m, 1 - c] = jnp.where(c == 0, w[:, :320], w[:, 64:])
+    for j in range(3):
+        s_swap(3 + j, zp[j]).wait()
+    nout[0:4, :] = NG[0]
+    tot = SQ[0] + SX[3] + SX[4] + SX[5]
+    nout[4:8, :] = jnp.zeros((4, D), f32) + jnp.sum(tot)
+    c_lg.wait()
+
+
+ORD = {5: 0, 4: 1, 3: 2, 0: 3, 1: 4, 2: 5}
+
+
+def run_block(sh, lat, cot, live, norms):
+    bf, f32 = jnp.bfloat16, jnp.float32
+    dma = pltpu.SemaphoreType.DMA
+    act = pltpu.VMEM((ROWS, D), bf)
+    wide = pltpu.VMEM((ROWS, D), f32)
+    vm, hbm = pl.BlockSpec(memory_space=pltpu.VMEM), pl.BlockSpec(memory_space=pl.ANY)
+    return pl.pallas_call(
+        block_kernel,
+        out_shape=(
+            jax.ShapeDtypeStruct((ROWS, D), bf),
+            jax.ShapeDtypeStruct((ROWS, D), bf),
+            jax.ShapeDtypeStruct((NM, 2, 80, 320), f32),
+            jax.ShapeDtypeStruct((8, D), f32),
+        ),
+        in_specs=[vm, hbm, hbm, pl.BlockSpec(memory_space=pltpu.SMEM), vm],
+        out_specs=(hbm, hbm, vm, vm),
+        scratch_shapes=[
+            pltpu.VMEM((7, 4, 2, 2, 80, D), bf), pltpu.VMEM((NM, 80, 320), bf),
+            act, act, act, act, act, act, pltpu.VMEM((16, LAT, LAT), bf), act, wide, act, act, act, wide,
+            pltpu.VMEM((RD_SLOTS, 4, 2, 80, D), bf), pltpu.VMEM((NM, 2, 4, 80, 640), bf),
+            pltpu.VMEM((NM, 4, 80, 640), bf), pltpu.VMEM((NM, 3, 80, 640), bf),
+            pltpu.VMEM((NM, 80, 384), f32), pltpu.VMEM((NM, 80, 384), f32),
+            pltpu.VMEM((1, 4, D), f32), pltpu.VMEM((6, 4, D), f32),
+            pltpu.VMEM((1, 8, 128), f32), pltpu.VMEM((6, 8, 128), f32),
+            dma((NM,)), dma((NM,)), dma((NM, 3)), dma((NM, 3)), dma((NM,)), dma((NM,)),
+            dma((NM,)), dma((NM,)), dma((NM,)), dma((NM,)),
+            dma((NM,)), dma((NM,)), dma((NM, 2)), dma((NM, 2)), dma((NM,)), dma((NM,)),
+            dma((NM, 3)), dma((NM, 3)), dma((NM,)), dma((NM,)), dma((6,)), dma((6,)),
+            dma((6,)), dma((6,)), dma((4,)), pltpu.SemaphoreType.REGULAR,
+        ],
+        compiler_params=pltpu.CompilerParams(
+            collective_id=0, has_side_effects=True, vmem_limit_bytes=64 * 1000 * 1000),
+        name="block",
+    )(sh.reshape(NM, 2, 80, 320), lat, cot, live, norms)
 
 
 def layer_norm(values, gain_row, bias_row):
@@ -101,22 +575,7 @@
     return (moment, square, update)
 
 
-def shards(
-    latents,
-    live_keys,
-    cotangent,
-    inner_weights,
-    outer_weights,
-    norm_params,
-    inner_first,
-    inner_second,
-    inner_average,
-    outer_first,
-    outer_second,
-    outer_average,
-    norm_first,
-    norm_second,
-):
+def plain(latents, live_keys, cotangent, inner_weights, outer_weights, norm_params):
     head_devices = lax.axis_size("head")
     data_devices = lax.axis_size("dp")
     row_count = latents.shape[0]
@@ -184,8 +643,43 @@
     norm_part = jnp.stack([grad_gain_one, grad_bias_one, grad_gain_two, grad_bias_two])
     local_squares = jnp.sum(grad_inner * grad_inner) + jnp.sum(grad_outer * grad_outer)
     grad_norms, squares_all = lax.psum((norm_part, local_squares), ("dp", "head"))
+    return block_output, latent_grad, grad_inner, grad_outer, grad_norms, squares_all
+
+
+def shards(
+    latents,
+    live_keys,
+    cotangent,
+    inner_weights,
+    outer_weights,
+    norm_params,
+    inner_first,
+    inner_second,
+    inner_average,
+    outer_first,
+    outer_second,
+    outer_average,
+    norm_first,
+    norm_second,
+):
+    head_devices = lax.axis_size("head")
+    data_devices = lax.axis_size("dp")
+    row_count = latents.shape[0]
+    token_total = row_count * head_devices * data_devices
+    if (data_devices, head_devices) == (8, 4):
+        sh = jnp.concatenate(
+            [inner_weights[:3], outer_weights[:1].swapaxes(1, 2), inner_weights[3:],
+             outer_weights[1:].swapaxes(1, 2)]).astype(jnp.bfloat16)
+        block_output, latent_grad, got, small = run_block(
+            sh, latents, cotangent, live_keys, norm_params)
+        got = got.reshape(NM, 160, 320)
+        grad_inner = jnp.stack([got[0], got[1], got[2], got[4]])
+        grad_outer = jnp.stack([got[3].T, got[5].T])
+        grad_norms, squares_all = small[:4], small[4, 0]
+    else:
+        block_output, latent_grad, grad_inner, grad_outer, grad_norms, squares_all = plain(
+            latents, live_keys, cotangent, inner_weights, outer_weights, norm_params)
     grad_norm = jnp.sqrt(squares_all + jnp.sum(grad_norms * grad_norms))
-    token_total = row_count * head_devices * data_devices
     clip_limit = CLIP_RATE * D * token_total**0.5
     factor = jnp.minimum(1.0, clip_limit / grad_norm)
     inner_rate = D ** (-0.5)

time: 838 us -> 265 us (0.32)
  waiting for transfers between devices: 503 us -> 0 us
  Pallas kernels: 0 us -> 238 us
  local copies, waits for them, and re-layouts: 158 us -> 8.48 us
  matrix products: 79.2 us -> 0 us
  blocking collectives: 39.6 us -> 0 us
  other arithmetic: 26.8 us -> 10.4 us
  between operations: 19.6 us -> 3.46 us
    pallas_call x0 -> x1, Pallas kernels: none -> 238 us  [run_block(): pl.pallas_call(block_kernel, out_shape=(jax.ShapeDtypeStruct((ROWS, D), b...]
    all_gather x4 -> x0, waiting for transfers between devices: 222 us -> none  [the longest x1 72.3 us: shards(): lax.all_gather(lax.all_gather(inner_weights.astype(jnp.bfloat16), 'dp', a...]
    unnamed x8 -> x0, waiting for transfers between devices: 184 us -> none
    reduce_scatter x2 -> x0, waiting for transfers between devices: 96.1 us -> none  [the longest x1 96 us: shards(): lax.psum_scatter(grad_inner.astype(jnp.bfloat16), 'head', scatter_dimensi...]
    dot_general x18 -> x0, matrix products: 79.2 us -> none  [the longest x1 11.7 us: shards(): jnp.einsum('trc,tdc->rd', d_proj, qkv_b, preferred_element_type=jnp.float32)]
    unnamed x88 -> x34, local copies, waits for them, and re-layouts: 50.4 us -> 4.95 us
    another operation x13 -> x0, local copies, waits for them, and re-layouts: 42.3 us -> none  [the longest x7 22 us: attend_back(): jnp.stack([d_query.reshape(flat_shape), d_key.reshape(flat_shape), d_valu...]
    psum x1 -> x0, blocking collectives: 39.6 us -> none  [shards(): lax.psum((norm_part, local_squares), ('dp', 'head'))]
  transfers between devices with their start and end apart: 7 -> 0, of which waited for: 6 -> 0; matrix products, arithmetic and copies ran while one was open for 15% -> 0% of each run, Pallas kernels for 0% -> 0%
where the time goes in v3:
time: 265 us; the launch traced here: 260 us
  Pallas kernels  238 us (90%)
  other arithmetic  10.4 us (4%)
  local copies, waits for them, and re-layouts  8.48 us (3%)
  between operations  3.46 us (1%)
    pallas_call x1, Pallas kernels, run_block(): pl.pallas_call(block_kernel, out_shape=(jax.ShapeDtypeStruct((ROWS, D), b...  238 us

profile of v3, /device:TPU:0, one launch (start us, length us, event | category | flops | bytes accessed | tf_op | source)
XLA Modules:
  0.0 260.3 jit_solution(10755214737263881083)
XLA Ops:
  0.7 0.0 copy-start
  0.7 1.1 convert.19
  1.8 0.2 copy-done
  2.0 0.1 convert.18
  2.1 1.0 pad_maximum_fusion.sh
  3.2 237.9 %block.1 = (bf16[512,1280]{1,0:T(8,128)(2,1)}, bf16[512,1280]{1,0:T(8,128)(2,1)}, f32[6,2,80,320]{3,2,1,0:T(8,128)}, f32[8,1280]{1,0:T(8,128)}) custom-call(bf16[6,2,80,320]{3,2,1,0:T(8,128)(2,1)} %pad_maximum_fusion.sh, bf16[512,1280]{1,0:T(8,128)(2,1)} %lat_in.1, bf16[512,1280]{1,0:T(8,128)(2,1)} %cot_in.1, s32[8]{0:T(128)} %live.1, f32[4,1280]{1,0:T(4,128)} %norms.1), custom_call_target="tpu_custom_call" | custom-call | tf_op jit(solution)/shard_map/block/pallas_call | solution.py:466
  241.1 1.4 multiply_reduce_fusion
  242.5 1.2 slice.61
  245.1 1.4 multiply_subtract_fusion.2
  246.6 0.6 slice.78
  247.2 1.7 fusion.8
  248.9 0.1 copy-done.9
  248.9 0.1 copy-done.10
  249.1 1.3 fusion.4
  250.4 0.0 copy-done.11
  250.4 0.9 multiply_add_fusion.3
  251.3 0.8 copy-done.7
  252.0 2.0 fusion.6
  254.1 1.1 multiply_add_fusion.1
  255.2 0.2 copy-done.1
  255.3 0.8 copy-done.5
  256.1 1.1 copy.34
  257.2 0.7 copy-done.4
  257.9 1.1 copy.35
  (26 shorter events, 0.1 us)
Async XLA Ops:
  0.7 1.4 copy-start
  3.2 241.9 %copy-start.12 = (f32[4,1280]{1,0:T(4,128)S(1)}, f32[4,1280]{1,0:T(4,128)}, u32[]{:S(2)}) copy-start(f32[4,1280]{1,0:T(4,128)} %norms.1) | copy-start | bytes 61444
  3.2 241.9 %copy-start.13 = (f32[4,1280]{1,0:T(4,128)S(1)}, f32[4,1280]{1,0:T(4,128)}, u32[]{:S(2)}) copy-start(f32[4,1280]{1,0:T(4,128)} %param.28) | copy-start | bytes 61444
  3.2 241.9 %copy-start.14 = (f32[4,1280]{1,0:T(4,128)S(1)}, f32[4,1280]{1,0:T(4,128)}, u32[]{:S(2)}) copy-start(f32[4,1280]{1,0:T(4,128)} %param.27) | copy-start | bytes 61444
  247.2 1.7 copy-start.2
  247.2 1.7 copy-start.9
  247.2 1.9 copy-start.10
  247.2 1.9 copy-start.15
  249.1 1.3 copy-start.11
  249.1 2.2 copy-start.8
  250.4 3.7 %copy-start.3 = (f32[2,320,160]{1,2,0:T(8,128)}, f32[2,320,160]{1,2,0:T(8,128)S(1)}, u32[]{:S(2)}) copy-start(f32[2,320,160]{1,2,0:T(8,128)S(1)} %get-tuple-element.72) | copy-start | bytes 1228804
  250.4 1.6 copy-start.7
  252.0 2.0 copy-start.6
  254.1 1.3 copy-start.1
  254.1 2.0 copy-start.5
  256.1 1.8 copy-start.4
